TPU v7x, 32 devices: a whole 2x2x4 slice. The times are simulated.
32 devices in a mesh: segment: 2 (over y), dp: 16 (over z, x, core).
Axes of the slice: x: 2, y: 2, z: 4, core: 2. Of those that a mesh axis runs over, the one named last changes fastest.
Arguments:
- segment_input: bfloat16 [2, 32, 384, 768], P('segment', 'dp'), may hold values from -16 to 16
- image_extent: int32 [32, 3], P('dp'), may hold values from 0 to 24, as said below
- norm1_gain: bfloat16 [2, 768], P('segment', 'dp'), may hold values from 0.5 to 1.5
- norm1_bias: bfloat16 [2, 768], P('segment', 'dp'), may hold values from -3 to 3
- norm2_gain: bfloat16 [2, 768], P('segment', 'dp'), may hold values from 0.5 to 1.5
- norm2_bias: bfloat16 [2, 768], P('segment', 'dp'), may hold values from -3 to 3
- qkv_weight: bfloat16 [2, 768, 2304], P('segment', 'dp'), may hold values from -0.21875 to 0.21875
- out_weight: bfloat16 [2, 768, 768], P('segment', 'dp'), may hold values from -1.75 to 1.75
- up_weight: bfloat16 [2, 768, 3072], P('segment', 'dp'), may hold values from -0.21875 to 0.21875
- down_weight: bfloat16 [2, 3072, 768], P('segment', 'dp'), may hold values from -0.109375 to 0.109375
- code_maps: bfloat16 [2, 768, 18], P('segment', 'dp'), may hold values from -1.5 to 1.5
Outputs:
- segment_output: float32 [2, 32, 384, 768], P('segment', 'dp')
- rms_stats: float32 [2, 3], P('segment')
- norm1_gain_grad: float32 [2, 768], P('segment', 'dp')
- norm1_bias_grad: float32 [2, 768], P('segment', 'dp')
- norm2_gain_grad: float32 [2, 768], P('segment', 'dp')
- norm2_bias_grad: float32 [2, 768], P('segment', 'dp')
- qkv_weight_grad: float32 [2, 768, 2304], P('segment', 'dp')
- out_weight_grad: float32 [2, 768, 768], P('segment', 'dp')
- up_weight_grad: float32 [2, 768, 3072], P('segment', 'dp')
- down_weight_grad: float32 [2, 3072, 768], P('segment', 'dp')
- code_maps_grad: float32 [2, 768, 18], P('segment', 'dp')
Inputs may be any that keep to these rules, and one draw needn't show every extreme that they name: `image_extent`: column 0 is the bucket: 0 for a grid of 16 rows of 24 patches, 1 for 24 rows of 16; patch p lies in row p // (row length) and column p % (row length). Columns 1 and 2 count the valid rows and columns, from a quarter of the bucket's (at least 1) up to all of them.
All inputs are finite; a program needn't handle non-finite values.
Results may differ from a plain program's by a relative error of at most 0.025.
Values may be sent and summed in bfloat16 or wider, within the bound.
A program may use at most 256 MiB of HBM per device.

v0:
```python
from functools import partial
import math

import jax
import jax.numpy as jnp
from jax import lax
from jax.sharding import PartitionSpec as P

HEADS = 12
CODE_BITS = 18
GH = 16
GW = 24
MB = 2


norm_eps = 1e-06


def passed_along(array, axis, by):
    length = lax.axis_size(axis)
    pairs = [(i, i + by) for i in range(length) if 0 <= i + by < length]
    return lax.ppermute(array, axis, pairs)


def layer_norm(values_in, norm_gain, norm_bias):
    centered = values_in - jnp.mean(values_in, -1, keepdims=True)
    return (
        centered
        * lax.rsqrt(jnp.mean(centered * centered, -1, keepdims=True) + norm_eps)
        * norm_gain
        + norm_bias
    )


def extent_mask(extent, patches):
    bucket = extent[:, 0:1]
    line_len = jnp.where(bucket == 0, GW, GH)
    position = jnp.arange(patches, dtype=jnp.int32)[None, :]
    inside = (position // line_len < extent[:, 1:2]) & (position % line_len < extent[:, 2:3])
    return inside.astype(jnp.float32)


def soft_code(code_pre):
    direction = code_pre * lax.rsqrt(jnp.sum(code_pre * code_pre, 0, keepdims=True) + 1.0)
    return jnp.tanh(2.0 * math.sqrt(code_pre.shape[0]) * direction)


def energy(tensor, row_mask):
    return jnp.sum(row_mask * jnp.sum(tensor * tensor, -1))


def split_heads(qkv_low, image_count, patches):
    head_dim = qkv_low.shape[1] // (3 * HEADS)
    joined = qkv_low.reshape(image_count, patches, 3, HEADS, head_dim)
    return (joined[:, :, 0], joined[:, :, 1], joined[:, :, 2])


def masked_scores(queries, key_rows, patch_keep_mask):
    head_dim = queries.shape[-1]
    scores = jnp.einsum(
        "iqhe,ikhe->ihqk", queries, key_rows, preferred_element_type=jnp.float32
    ) * (1.0 / math.sqrt(head_dim))
    return jnp.where(patch_keep_mask[:, None, None, :] > 0, scores, -1e30)


def attention_forward(block_in, patch_keep_mask, weights):
    norm_gain, norm_bias, w_qkv, w_out = weights
    image_count, patches = patch_keep_mask.shape
    features = block_in.shape[1]
    normed = layer_norm(block_in, norm_gain, norm_bias).astype(jnp.bfloat16)
    qkv_low = jnp.dot(normed, w_qkv, preferred_element_type=jnp.float32).astype(jnp.bfloat16)
    queries, key_rows, values = split_heads(qkv_low, image_count, patches)
    scores = masked_scores(queries, key_rows, patch_keep_mask)
    row_max = jnp.max(scores, -1, keepdims=True)
    exponent = jnp.exp(scores - row_max)
    row_sum = jnp.sum(exponent, -1, keepdims=True)
    probs_low = (exponent / row_sum).astype(jnp.bfloat16)
    log_total = (row_max + jnp.log(row_sum))[..., 0]
    mixed_heads = jnp.einsum(
        "ihqk,ikhe->iqhe", probs_low, values, preferred_element_type=jnp.float32
    )
    mixed_heads = mixed_heads.reshape(image_count * patches, features).astype(jnp.bfloat16)
    attn_out = jnp.dot(mixed_heads, w_out, preferred_element_type=jnp.float32)
    return (attn_out, qkv_low, log_total, mixed_heads)


def mlp_forward(middle, weights):
    norm_gain, norm_bias, w_up, w_down = weights
    normed = layer_norm(middle, norm_gain, norm_bias).astype(jnp.bfloat16)
    pre_act = jnp.dot(normed, w_up, preferred_element_type=jnp.float32)
    activation = jax.nn.gelu(pre_act, approximate=False).astype(jnp.bfloat16)
    return (jnp.dot(activation, w_down, preferred_element_type=jnp.float32), pre_act)


def block_forward(block_in, patch_keep_mask, attn_weights, mlp_weights):
    attn_out, qkv_low, log_total, mixed_heads = attention_forward(
        block_in, patch_keep_mask, attn_weights
    )
    middle = block_in + attn_out
    mlp_out, pre_act = mlp_forward(middle, mlp_weights)
    block_result = middle + mlp_out
    row_mask = patch_keep_mask.reshape(-1)
    energies = jnp.stack(
        [energy(block_result, row_mask), energy(attn_out, row_mask), energy(mlp_out, row_mask)]
    )
    return (block_result, (block_in, qkv_low, log_total, mixed_heads, middle, pre_act), energies)


def blank_forward(block_in, patch_keep_mask, attn_weights, mlp_weights):
    row_total, features = block_in.shape
    image_count, patches = patch_keep_mask.shape
    hidden = mlp_weights[2].shape[1]
    zero_rows = jnp.zeros((row_total, features), jnp.float32)
    saved_tensor = (
        zero_rows,
        jnp.zeros((row_total, 3 * features), jnp.bfloat16),
        jnp.zeros((image_count, HEADS, patches), jnp.float32),
        jnp.zeros((row_total, features), jnp.bfloat16),
        zero_rows,
        jnp.zeros((row_total, hidden), jnp.float32),
    )
    return (zero_rows, saved_tensor, jnp.zeros((3,), jnp.float32))


def mlp_backward(grad_out, middle, pre_act, weights):
    norm_gain, norm_bias, w_up, w_down = weights
    grad_low = grad_out.astype(jnp.bfloat16)
    activation, gelu_back = jax.vjp(partial(jax.nn.gelu, approximate=False), pre_act)
    grad_act = jnp.einsum("rd,fd->rf", grad_low, w_down, preferred_element_type=jnp.float32)
    grad_pre = gelu_back(grad_act)[0].astype(jnp.bfloat16)
    normed, norm_back = jax.vjp(
        layer_norm, middle, norm_gain.astype(jnp.float32), norm_bias.astype(jnp.float32)
    )
    grad_normed = jnp.einsum("rf,df->rd", grad_pre, w_up, preferred_element_type=jnp.float32)
    grad_part, gain_grad, bias_grad = norm_back(grad_normed)
    operands = (activation.astype(jnp.bfloat16), grad_low, normed.astype(jnp.bfloat16), grad_pre)
    return (grad_out + grad_part, (gain_grad, bias_grad), operands)


def blank_mlp(grad_out, middle, pre_act, weights):
    row_total, features = grad_out.shape
    hidden = weights[2].shape[1]
    operands = (
        jnp.zeros((row_total, hidden), jnp.bfloat16),
        jnp.zeros((row_total, features), jnp.bfloat16),
        jnp.zeros((row_total, features), jnp.bfloat16),
        jnp.zeros((row_total, hidden), jnp.bfloat16),
    )
    return (
        jnp.zeros_like(grad_out),
        (jnp.zeros((features,), jnp.float32), jnp.zeros((features,), jnp.float32)),
        operands,
    )


def mlp_weight_grads(operands):
    activation_low, grad_low, normed_low, grad_pre = operands
    up_grad = jnp.einsum("rd,rf->df", normed_low, grad_pre, preferred_element_type=jnp.float32)
    down_grad = jnp.einsum(
        "rf,rd->fd", activation_low, grad_low, preferred_element_type=jnp.float32
    )
    return (up_grad, down_grad)


def attention_backward(
    grad_mid, block_in, qkv_low, log_total, mixed_heads, patch_keep_mask, weights
):
    norm_gain, norm_bias, w_qkv, w_out = weights
    image_count, patches = patch_keep_mask.shape
    features = block_in.shape[1]
    head_dim = features // HEADS
    grad_low = grad_mid.astype(jnp.bfloat16)
    grad_mixed = jnp.einsum(
        "re,de->rd", grad_low, w_out, preferred_element_type=jnp.float32
    ).astype(jnp.bfloat16)
    grad_mixed = grad_mixed.reshape(image_count, patches, HEADS, head_dim)
    queries, key_rows, values = split_heads(qkv_low, image_count, patches)
    scores = masked_scores(queries, key_rows, patch_keep_mask)
    probs = jnp.exp(scores - log_total[..., None])
    grad_probs = jnp.einsum(
        "iqhe,ikhe->ihqk", grad_mixed, values, preferred_element_type=jnp.float32
    )
    grad_values = jnp.einsum(
        "ihqk,iqhe->ikhe",
        probs.astype(jnp.bfloat16),
        grad_mixed,
        preferred_element_type=jnp.float32,
    )
    inner = jnp.sum(probs * grad_probs, -1, keepdims=True)
    grad_scores = (probs * (grad_probs - inner)).astype(jnp.bfloat16)
    score_scale = 1.0 / math.sqrt(head_dim)
    grad_queries = (
        jnp.einsum("ihqk,ikhe->iqhe", grad_scores, key_rows, preferred_element_type=jnp.float32)
        * score_scale
    )
    grad_keys = (
        jnp.einsum("ihqk,iqhe->ikhe", grad_scores, queries, preferred_element_type=jnp.float32)
        * score_scale
    )
    grad_qkv = (
        jnp.stack([grad_queries, grad_keys, grad_values], 2)
        .astype(jnp.bfloat16)
        .reshape(image_count * patches, 3 * features)
    )
    normed, norm_back = jax.vjp(
        layer_norm, block_in, norm_gain.astype(jnp.float32), norm_bias.astype(jnp.float32)
    )
    grad_normed = jnp.einsum("re,de->rd", grad_qkv, w_qkv, preferred_element_type=jnp.float32)
    grad_part, gain_grad, bias_grad = norm_back(grad_normed)
    operands = (mixed_heads, grad_low, normed.astype(jnp.bfloat16), grad_qkv)
    return (grad_mid + grad_part, (gain_grad, bias_grad), operands)


def blank_attention(grad_mid, block_in, qkv_low, log_total, mixed_heads, patch_keep_mask, weights):
    row_total, features = grad_mid.shape
    operands = (
        jnp.zeros((row_total, features), jnp.bfloat16),
        jnp.zeros((row_total, features), jnp.bfloat16),
        jnp.zeros((row_total, features), jnp.bfloat16),
        jnp.zeros((row_total, 3 * features), jnp.bfloat16),
    )
    return (
        jnp.zeros_like(grad_mid),
        (jnp.zeros((features,), jnp.float32), jnp.zeros((features,), jnp.float32)),
        operands,
    )


def attention_weight_grads(operands):
    mixed_heads, grad_low, normed_low, grad_qkv = operands
    qkv_grad = jnp.einsum("rd,re->de", normed_low, grad_qkv, preferred_element_type=jnp.float32)
    out_grad = jnp.einsum("rd,re->de", mixed_heads, grad_low, preferred_element_type=jnp.float32)
    return (qkv_grad, out_grad)


def join_rows(pieces):
    return jax.tree.map(lambda *members: jnp.concatenate(members, 0), *pieces)


def on_device(
    segment_input,
    image_extent,
    norm1_gain,
    norm1_bias,
    norm2_gain,
    norm2_bias,
    qkv_weight,
    out_weight,
    up_weight,
    down_weight,
    code_maps,
):
    segment_no = lax.axis_index("segment")
    is_first = segment_no == 0
    images = segment_input.shape[1]
    patches = segment_input.shape[2]
    features = segment_input.shape[3]
    microbatch_count = MB
    per_micro = images // microbatch_count
    row_total = per_micro * patches
    validity = extent_mask(image_extent, patches)
    own_input = segment_input[0]
    attn_set = (
        lax.all_gather(norm1_gain, "dp", axis=1, tiled=True),
        lax.all_gather(norm1_bias, "dp", axis=1, tiled=True),
        lax.all_gather(qkv_weight, "dp", axis=1, tiled=True),
        lax.all_gather(out_weight, "dp", axis=1, tiled=True),
        lax.all_gather(code_maps, "dp", axis=1, tiled=True),
    )
    attn_weights = tuple((member[0] for member in attn_set))
    mlp_set = (
        lax.all_gather(norm2_gain, "dp", axis=1, tiled=True),
        lax.all_gather(norm2_bias, "dp", axis=1, tiled=True),
        lax.all_gather(up_weight, "dp", axis=1, tiled=True),
        lax.all_gather(down_weight, "dp", axis=1, tiled=True),
    )
    mlp_weights = tuple((member[0] for member in mlp_set))
    code_in = jnp.zeros((CODE_BITS, row_total), jnp.bfloat16)
    code_grad = jnp.zeros((CODE_BITS, row_total), jnp.bfloat16)
    energies = jnp.zeros((3,), jnp.float32)
    saved_tensors = []
    decoded = []
    pieces = []
    for step_index in range(microbatch_count + 1):
        run_send = step_index < microbatch_count
        run_position = step_index - segment_no
        run_active = (run_position >= 0) & (run_position < microbatch_count)
        run_start_at = jnp.clip(run_position, 0, microbatch_count - 1) * per_micro
        inputs = (
            lax.dynamic_slice_in_dim(own_input, run_start_at, per_micro, 0)
            .reshape(row_total, features)
            .astype(jnp.float32)
        )
        run_patch_keep_mask = lax.dynamic_slice_in_dim(validity, run_start_at, per_micro, 0)
        lifted = jnp.einsum(
            "lr,dl->rd", code_in, attn_weights[4], preferred_element_type=jnp.float32
        )
        block_in = jnp.where(is_first, inputs, lifted)
        run_block_result, run_saved_tensor, part_energy = lax.cond(
            run_active,
            block_forward,
            blank_forward,
            block_in,
            run_patch_keep_mask,
            attn_weights[:4],
            mlp_weights,
        )
        run_code_pre = jnp.einsum(
            "rd,dl->lr",
            run_block_result.astype(jnp.bfloat16),
            attn_weights[4],
            preferred_element_type=jnp.float32,
        )
        codes_out = soft_code(run_code_pre).astype(jnp.bfloat16)
        run_record_item = (run_saved_tensor, code_in, run_patch_keep_mask, run_block_result)
        run_code_next = code_in
        if run_send:
            run_code_next = passed_along(codes_out, "segment", 1)
        record_item, part_energy, code_in = (run_record_item, part_energy, run_code_next)
        energies = energies + part_energy
        saved_tensors.append(record_item)
        decoded.append(record_item[3])
    weight_pair = (attn_weights, mlp_weights)
    attn_use, mlp_use = weight_pair
    mlp_shards = (
        jnp.zeros(norm2_gain.shape, jnp.float32),
        jnp.zeros(norm2_bias.shape, jnp.float32),
        jnp.zeros(up_weight.shape, jnp.float32),
        jnp.zeros(down_weight.shape, jnp.float32),
    )
    attn_shards = (
        jnp.zeros(norm1_gain.shape, jnp.float32),
        jnp.zeros(norm1_bias.shape, jnp.float32),
        jnp.zeros(qkv_weight.shape, jnp.float32),
        jnp.zeros(out_weight.shape, jnp.float32),
        jnp.zeros(code_maps.shape, jnp.float32),
    )
    small_total = (
        jnp.zeros((features,), jnp.float32),
        jnp.zeros((features,), jnp.float32),
        jnp.zeros((features,), jnp.float32),
        jnp.zeros((features,), jnp.float32),
        jnp.zeros(attn_use[4].shape, jnp.float32),
    )
    sums = (mlp_shards, attn_shards, small_total, [], [])
    results = []
    for step_index in range(microbatch_count + 1):
        position = microbatch_count - step_index - segment_no
        run_attn_use, run_mlp_use = weight_pair
        run_mlp_shards, run_attn_shards, run_small_total, mlp_pieces, attn_pieces = sums
        code_maps_all = run_attn_use[4]
        saved_tensor, applied_code, patch_keep_mask, block_result = saved_tensors[
            microbatch_count - step_index
        ]
        active = (position >= 0) & (position < microbatch_count)
        start_at = jnp.clip(position, 0, microbatch_count - 1) * per_micro
        target = (
            lax.dynamic_slice_in_dim(own_input, start_at, per_micro, 0)
            .reshape(row_total, features)
            .astype(jnp.float32)
        )
        out_low = block_result.astype(jnp.bfloat16)
        code_pre = jnp.einsum(
            "rd,dl->lr", out_low, code_maps_all, preferred_element_type=jnp.float32
        )
        code_value, code_back = jax.vjp(soft_code, code_pre)
        grad_code = code_back(code_grad.astype(jnp.float32))[0].astype(jnp.bfloat16)
        enc_grad = jnp.einsum(
            "lr,dl->rd", grad_code, code_maps_all, preferred_element_type=jnp.float32
        )
        grad_out = jnp.where(is_first, enc_grad, target)
        enc_map = jnp.einsum("rd,lr->dl", out_low, grad_code, preferred_element_type=jnp.float32)
        map_part = jnp.where(is_first & active, enc_map, 0.0)
        grad_mid, mlp_small, mlp_operands = lax.cond(
            active, mlp_backward, blank_mlp, grad_out, saved_tensor[4], saved_tensor[5], run_mlp_use
        )
        mlp_pieces = mlp_pieces + [mlp_operands]
        grad_in, attn_small, attn_operands = lax.cond(
            active,
            attention_backward,
            blank_attention,
            grad_mid,
            saved_tensor[0],
            saved_tensor[1],
            saved_tensor[2],
            saved_tensor[3],
            patch_keep_mask,
            run_attn_use[:4],
        )
        grad_in_low = grad_in.astype(jnp.bfloat16)
        dec_map = jnp.einsum(
            "rd,lr->dl", grad_in_low, applied_code, preferred_element_type=jnp.float32
        )
        map_part = map_part + jnp.where(jnp.logical_not(is_first) & active, dec_map, 0.0)
        code_grad_new = jnp.einsum(
            "rd,dl->lr", grad_in_low, code_maps_all, preferred_element_type=jnp.float32
        ).astype(jnp.bfloat16)
        code_next = code_grad
        if step_index < microbatch_count:
            code_next = passed_along(code_grad_new, "segment", -1)
        attn_pieces = attn_pieces + [attn_operands]
        run_small_total = jax.tree.map(
            jnp.add,
            run_small_total,
            (mlp_small[0], mlp_small[1], attn_small[0], attn_small[1], map_part),
        )
        if step_index == microbatch_count:
            up_grad, down_grad = mlp_weight_grads(join_rows(mlp_pieces))
            run_mlp_shards = (
                lax.psum_scatter(run_small_total[0][None], "dp", scatter_dimension=1, tiled=True),
                lax.psum_scatter(run_small_total[1][None], "dp", scatter_dimension=1, tiled=True),
                lax.psum_scatter(up_grad[None], "dp", scatter_dimension=1, tiled=True),
                lax.psum_scatter(down_grad[None], "dp", scatter_dimension=1, tiled=True),
            )
            qkv_grad, out_grad = attention_weight_grads(join_rows(attn_pieces))
            run_attn_shards = (
                lax.psum_scatter(run_small_total[2][None], "dp", scatter_dimension=1, tiled=True),
                lax.psum_scatter(run_small_total[3][None], "dp", scatter_dimension=1, tiled=True),
                lax.psum_scatter(qkv_grad[None], "dp", scatter_dimension=1, tiled=True),
                lax.psum_scatter(out_grad[None], "dp", scatter_dimension=1, tiled=True),
                lax.psum_scatter(run_small_total[4][None], "dp", scatter_dimension=1, tiled=True),
            )
        grad_in, code_grad, sums = (
            grad_in,
            code_next,
            (run_mlp_shards, run_attn_shards, run_small_total, mlp_pieces, attn_pieces),
        )
        results.append(grad_in)
    for micro_index in range(microbatch_count):
        chosen = jnp.where(
            is_first, results[microbatch_count - micro_index], decoded[micro_index + 1]
        )
        pieces.append(chosen.reshape(per_micro, patches, features))
    mlp_shards, attn_shards = (sums[0], sums[1])
    segment_output = jnp.concatenate(pieces, 0)[None]
    energy_all, valid_all = lax.psum((energies, jnp.sum(validity)), "dp")
    rms_stats = jnp.sqrt(energy_all / (valid_all * features))[None]
    return (
        segment_output,
        rms_stats,
        attn_shards[0],
        attn_shards[1],
        mlp_shards[0],
        mlp_shards[1],
        attn_shards[2],
        attn_shards[3],
        mlp_shards[2],
        mlp_shards[3],
        attn_shards[4],
    )


def solution(mesh):
    return jax.shard_map(
        on_device,
        mesh=mesh,
        in_specs=(
            P("segment", "dp", None, None),
            P("dp", None),
            P("segment", "dp"),
            P("segment", "dp"),
            P("segment", "dp"),
            P("segment", "dp"),
            P("segment", "dp", None),
            P("segment", "dp", None),
            P("segment", "dp", None),
            P("segment", "dp", None),
            P("segment", "dp", None),
        ),
        out_specs=(
            P("segment", "dp", None, None),
            P("segment", None),
            P("segment", "dp"),
            P("segment", "dp"),
            P("segment", "dp"),
            P("segment", "dp"),
            P("segment", "dp", None),
            P("segment", "dp", None),
            P("segment", "dp", None),
            P("segment", "dp", None),
            P("segment", "dp", None),
        ),
        check_vma=False,
    )
```

profile of v0, /device:TPU:0, one launch (start us, length us, event | category | flops | bytes accessed | tf_op | source)
XLA Modules:
  0.0 1265.7 jit_solution(6262765017244565416)
XLA Ops:
  10.8 24.3 %all_gather.27 = bf16[1,768,18]{2,0,1:T(2,128)(2,1)S(1)} all-gather(bf16[1,48,18]{2,0,1:T(2,128)(2,1)S(1)} %copy.137), channel_id=1, replica_groups=mesh['segment'=2,'dp'=16] {'dp'}, dimensions={1}, use_global_device_ids=true | all-gather | bytes 29376 | tf_op jit(solution)/shard_map/all_gather | solution.py:268
  40.7 30.6 %all-reduce.5 = (bf16[768]{0:T(1024)(128)(2,1)S(1)}, bf16[768]{0:T(1024)(128)(2,1)S(1)}, bf16[768]{0:T(1024)(128)(2,1)S(1)}, bf16[768]{0:T(1024)(128)(2,1)S(1)}) all-reduce(bf16[768]{0:T(1024)(128)(2,1)S(1)} %dynamic-update-slice, bf16[768]{0:T(1024)(128)(2,1)S(1)} %dynamic-update-slice.1, ...), channel_id=1, replica_groups=mesh['segment'=2,'dp'=16] {'dp'}, use_global_device_ids=true, to_apply=%add | all-reduce | flops 3072 | bytes 12288 | tf_op jit(solution)/shard_map/squeeze | solution.py:270
  78.2 21.9 %all-gather.5.cloned.1.call-done = bf16[1,768,2304]{2,1,0:T(8,128)(2,1)} async-done(((bf16[1,48,2304]{2,1,0:T(8,128)(2,1)}), bf16[1,768,2304]{2,1,0:T(8,128)(2,1)}) %all-gather.5.cloned.1.call-update) | async-done | bytes 3538960 | tf_op jit(solution)/shard_map/all_gather | solution.py:266
  100.1 54.6 %all-gather.9.cloned.1.call-done = bf16[1,768,3072]{2,1,0:T(8,128)(2,1)} async-done(((bf16[1,48,3072]{2,1,0:T(8,128)(2,1)}), bf16[1,768,3072]{2,1,0:T(8,128)(2,1)}) %all-gather.9.cloned.1.call-update) | async-done | bytes 4718608 | tf_op jit(solution)/shard_map/all_gather | solution.py:274
  154.7 54.0 %all-gather.11.cloned.1.call-done = bf16[1,3072,768]{2,1,0:T(8,128)(2,1)} async-done(((bf16[1,192,768]{2,1,0:T(8,128)(2,1)}), bf16[1,3072,768]{2,1,0:T(8,128)(2,1)}) %all-gather.11.cloned.1.call-update) | async-done | bytes 4718608 | tf_op jit(solution)/shard_map/all_gather | solution.py:275
  208.7 45.8 %conditional.9 = (f32[384,768]{1,0:T(8,128)}, bf16[384,2304]{1,0:T(8,128)(2,1)}, f32[1,12,384]{2,1,0:T(8,128)S(1)}, bf16[384,768]{0,1:T(8,128)(2,1)}, f32[384,76...) conditional(s32[]{:T(128)} %convert_element_type.372, () %tuple.91, ...), branch_computations={%region_0.1_spmd, %region_1.14_spmd} | conditional | flops 5996151296 | bytes 117616488 | solution.py:299
  214.1 3.9 copy.117
  222.7 4.1 fusion.39
  231.4 5.6 fusion.40
  237.0 14.6 %multiply_reduce_fusion.11 = (f32[384]{0:T(512)S(1)}, f32[384]{0:T(512)S(1)}, bf16[384,768]{1,0:T(8,128)(2,1)}) fusion(f32[384,768]{1,0:T(8,128)} %get-tuple-element.851, bf16[3072,768]{1,0:T(8,128)(2,1)S(1)} %bitcast.429, f32[384,3072]{1,0:T(8,128)} %fusion.40), kind=kOutput, calls=%fused_computation.120 | convolution fusion | flops 1890385152 | bytes 11209728 | tf_op jit(solution)/shard_map/cond/branch_1_fun/dot_general | solution.py:92
  261.0 45.3 %conditional.10 = (f32[384,768]{1,0:T(8,128)}, f32[384,768]{1,0:T(8,128)S(1)}, bf16[384,2304]{1,0:T(8,128)(2,1)}, f32[1,12,384]{2,1,0:T(8,128)S(1)}, bf16[384,76...) conditional(s32[]{:T(128)} %convert_element_type.376, () %tuple.95, ...), branch_computations={%region_15.16_spmd, %region_16.29_spmd} | conditional | flops 5996151296 | bytes 127053760 | solution.py:299
  281.8 5.6 fusion.98
  287.4 14.9 %fusion.360 = (bf16[384,768]{1,0:T(8,128)(2,1)S(1)}, f32[384,768]{1,0:T(8,128)}, f32[384]{0:T(512)S(1)}) fusion(f32[384,768]{1,0:T(8,128)} %get-tuple-element.869, bf16[3072,768]{1,0:T(8,128)(2,1)S(1)} %bitcast.431, f32[384,3072]{1,0:T(8,128)} %fusion.98), kind=kOutput, calls=%fused_computation.624 | convolution fusion | flops 1889795712 | bytes 12387840 | tf_op jit(solution)/shard_map/cond/branch_1_fun/dot_general | solution.py:92
  309.2 4.1 collective-permute-start.1
  315.9 14.1 %conditional.11 = (f32[384,768]{1,0:T(8,128)}, f32[384,768]{1,0:T(8,128)S(1)}, bf16[384,2304]{1,0:T(8,128)(2,1)}, f32[1,12,384]{2,1,0:T(8,128)S(1)}, bf16[384,76...) conditional(s32[]{:T(128)} %convert_element_type.380, () %tuple.99, ...), branch_computations={%region_30.31_spmd, %region_31.44_spmd} | conditional | flops 5996151296 | bytes 124694432 | solution.py:299
  335.6 7.4 conditional.12
  343.0 15.4 %conditional.13 = (f32[768]{0:T(1024)}, f32[768]{0:T(1024)}, bf16[384,768]{1,0:T(8,128)(2,1)}, bf16[384,768]{1,0:T(8,128)(2,1)}, bf16[384,768]{1,0:T(8,128)(2,1)...) conditional(s32[]{:T(128)} %convert_element_type.380, () %tuple.98, (f32[384,768]{1,0:T(8,128)S(1)}, ...), branch_computations={%region_54.55_spmd, %region_55.63_spmd} | conditional | flops 2982443264 | bytes 122913984 | solution.py:378
  363.0 89.2 %collective-permute-done.2 = bf16[18,384]{1,0:T(8,128)(2,1)S(1)} collective-permute-done((bf16[18,384]{1,0:T(8,128)(2,1)S(1)}, bf16[18,384]{1,0:T(8,128)(2,1)S(1)}, u32[]{:S(2)}, u32[]{:S(2)}) %collective-permute-start.2) | collective-permute-done | bytes 13856 | tf_op jit(solution)/shard_map/ppermute | solution.py:22
  458.5 31.7 %conditional.14 = (f32[384,768]{1,0:T(8,128)S(1)}, f32[768]{0:T(1024)}, f32[768]{0:T(1024)}, bf16[384,3072]{1,0:T(8,128)(2,1)}, bf16[384,768]{1,0:T(8,128)(2,1)}...) conditional(s32[]{:T(128)} %convert_element_type.376, () %tuple.97, (pred[]{:T(512)}, ...), branch_computations={%region_64.65_spmd, %region_65.72_spmd} | conditional | flops 3725036288 | bytes 85579952 | solution.py:374
  463.9 12.2 multiply_convert_fusion.1
  476.1 6.1 add_convert_fusion.2
  482.3 4.9 multiply_reduce_fusion.3
  491.2 39.3 %conditional.15 = (f32[384,768]{1,0:T(8,128)}, f32[768]{0:T(1024)S(1)}, f32[768]{0:T(1024)S(1)}, bf16[384,768]{1,0:T(8,128)(2,1)}, bf16[384,768]{1,0:T(8,128)(2,...) conditional(s32[]{:T(128)} %convert_element_type.376, () %tuple.94, ...), branch_computations={%region_72.73_spmd, %region_73.81_spmd} | conditional | flops 2982443264 | bytes 133555512 | solution.py:378
  491.2 3.9 copy.141
  495.2 5.4 fusion.232
  506.1 6.0 multiply_reduce_fusion.37
  520.5 5.1 multiply_reduce_fusion.38
  544.5 34.2 %conditional.16 = (f32[384,768]{1,0:T(8,128)}, f32[768]{0:T(1024)}, f32[768]{0:T(1024)}, bf16[384,3072]{1,0:T(8,128)(2,1)}, bf16[384,768]{1,0:T(8,128)(2,1)}, /*...) conditional(s32[]{:T(128)} %convert_element_type.372, () %tuple.93, (pred[]{:T(512)}, f32[384,768]{1,0:T(8,128)}, ...), branch_computations={%region_82.83_spmd, %region_83.90_spmd} | conditional | flops 3725036288 | bytes 85579952 | solution.py:374
  551.2 12.1 multiply_convert_fusion.2
  563.4 6.1 add_convert_fusion.4
  569.5 4.9 multiply_reduce_fusion.6
  582.0 38.3 %conditional.17 = (f32[384,768]{1,0:T(8,128)S(1)}, f32[768]{0:T(1024)S(1)}, f32[768]{0:T(1024)S(1)}, bf16[384,768]{1,0:T(8,128)(2,1)}, bf16[384,768]{1,0:T(8,128...) conditional(s32[]{:T(128)} %convert_element_type.372, () %tuple.90, (f32[1,384]{1,0:T(1,128)}, ...), branch_computations={%region_90.91_spmd, %region_91.99_spmd} | conditional | flops 2982148352 | bytes 118785184 | solution.py:378
  582.1 3.9 copy.143
  586.0 5.3 fusion.251
  596.2 6.0 multiply_reduce_fusion.41
  610.8 4.4 multiply_reduce_fusion.42
  626.1 5.2 fusion.304
  631.3 10.8 convolution_bitcast_fusion
  642.2 11.3 fusion.270
  653.8 11.3 fusion.267
  665.8 30.2 %all-reduce.4 = (f32[3]{0:T(128)S(1)}, f32[]{:T(128)}) all-reduce(f32[3]{0:T(128)S(1)} %add_add_fusion.18, f32[]{:T(128)} %get-tuple-element.789), channel_id=1, replica_groups=mesh['segment'=2,'dp'=16] {'dp'}, use_global_device_ids=true, to_apply=%region_99.100 | all-reduce | flops 4 | bytes 32 | tf_op jit(solution)/shard_map/psum | solution.py:436
  702.9 47.4 %reduce-scatter.30.cloned.1.call-done = f32[48,1]{1,0:T(8,128)} async-done(((f32[768,1]{1,0:T(8,128)}), f32[48,1]{1,0:T(8,128)}) %reduce-scatter.30.cloned.1.call-update) | async-done | bytes 208
  751.6 57.2 %reduce-scatter.28.cloned.1.call-done = f32[48,1]{1,0:T(8,128)} async-done(((f32[768,1]{1,0:T(8,128)}), f32[48,1]{1,0:T(8,128)}) %reduce-scatter.28.cloned.1.call-update) | async-done | bytes 208
  810.1 56.8 %reduce-scatter.36.cloned.1.call-done = f32[48,18]{1,0:T(8,128)} async-done(((f32[768,18]{1,0:T(8,128)}), f32[48,18]{1,0:T(8,128)}) %reduce-scatter.36.cloned.1.call-update) | async-done | bytes 3472
  868.3 65.3 %reduce-scatter.22.cloned.1.call-done = f32[1,48,768]{2,1,0:T(8,128)} async-done(((f32[1,768,768]{2,1,0:T(8,128)}), f32[1,48,768]{2,1,0:T(8,128)}) %reduce-scatter.22.cloned.1.call-update) | async-done | bytes 147472 | tf_op jit(solution)/shard_map/reduce_scatter | solution.py:420
  933.6 93.6 %reduce-scatter.20.cloned.1.call-done = f32[1,48,2304]{2,1,0:T(8,128)} async-done(((f32[1,768,2304]{2,1,0:T(8,128)}), f32[1,48,2304]{2,1,0:T(8,128)}) %reduce-scatter.20.cloned.1.call-update) | async-done | bytes 442384 | tf_op jit(solution)/shard_map/reduce_scatter | solution.py:419
  1027.2 116.0 %reduce-scatter.26.cloned.1.call-done = f32[1,192,768]{2,1,0:T(8,128)} async-done(((f32[1,3072,768]{2,1,0:T(8,128)}), f32[1,192,768]{2,1,0:T(8,128)}) %reduce-scatter.26.cloned.1.call-update) | async-done | bytes 589840 | tf_op jit(solution)/shard_map/reduce_scatter | solution.py:413
  1143.2 115.8 %reduce-scatter.24.cloned.1.call-done = f32[1,48,3072]{2,1,0:T(8,128)} async-done(((f32[1,768,3072]{2,1,0:T(8,128)}), f32[1,48,3072]{2,1,0:T(8,128)}) %reduce-scatter.24.cloned.1.call-update) | async-done | bytes 589840 | tf_op jit(solution)/shard_map/reduce_scatter | solution.py:412
  (388 shorter events, 198.5 us)
Async XLA Ops:
  7.2 71.0 %all-gather.7.cloned.1.call-start = ((), (), s32[]{:S(2)}) async-start(), calls=%async_computation.10 | async-start | bytes 1253376 | tf_op jit(solution)/shard_map/all_gather | solution.py:267
  7.9 92.2 %all-gather.5.cloned.1.call-start = ((), (), s32[]{:S(2)}) async-start(), calls=%async_computation.9 | async-start | bytes 3760128 | tf_op jit(solution)/shard_map/all_gather | solution.py:266
  8.7 146.0 %all-gather.9.cloned.1.call-start = ((), (), s32[]{:S(2)}) async-start(), calls=%async_computation.11 | async-start | bytes 5013504 | tf_op jit(solution)/shard_map/all_gather | solution.py:274
  9.4 199.2 %all-gather.11.cloned.1.call-start = ((), (), s32[]{:S(2)}) async-start(), calls=%async_computation.12 | async-start | bytes 5013504 | tf_op jit(solution)/shard_map/all_gather | solution.py:275
  10.0 690.3 %reduce-scatter.34.cloned.1.call-start = ((), (), s32[]{:S(2)}) async-start(), calls=%async_computation.20 | async-start | bytes 417792
  35.4 173.2 %copy-start.28 = (bf16[1,768,18]{1,2,0:T(8,128)(2,1)}, bf16[1,768,18]{1,2,0:T(8,128)(2,1)S(1)}, u32[]{:S(2)}) copy-start(bf16[1,768,18]{1,2,0:T(8,128)(2,1)S(1)} %copy.138) | copy-start | bytes 82948
  76.7 131.9 %copy-start.8 = (f32[384,768]{1,0:T(8,128)}, f32[384,768]{1,0:T(8,128)S(1)}, u32[]{:S(2)}) copy-start(f32[384,768]{1,0:T(8,128)S(1)} %get-tuple-element.822) | copy-start | bytes 3538948
  209.0 17.8 %copy-start.6 = (f32[384,768]{1,0:T(8,128)}, f32[384,768]{1,0:T(8,128)S(1)}, u32[]{:S(2)}) copy-start(f32[384,768]{1,0:T(8,128)S(1)} %get-tuple-element.847) | copy-start | bytes 3538948 | tf_op jit(solution)/shard_map/cond
  211.2 6.8 copy-start.56
  221.2 10.2 slice-start.6
  222.7 8.6 slice-start.7
  229.6 7.3 slice-start.18
  237.0 14.6 %copy-start.49 = (f32[384]{0:T(512)S(1)}, f32[384]{0:T(512)}, u32[]{:S(2)}) copy-start(f32[384]{0:T(512)} %copy-done.48) | copy-start | bytes 4612 | tf_op jit(solution)/shard_map/cond
  257.1 2.7 collective-permute-start
  261.2 17.0 %copy-start = (f32[384,768]{1,0:T(8,128)}, f32[384,768]{1,0:T(8,128)S(1)}, u32[]{:S(2)}) copy-start(f32[384,768]{1,0:T(8,128)S(1)} %get-tuple-element.865) | copy-start | bytes 3538948 | tf_op jit(solution)/shard_map/cond
  263.4 6.8 copy-start.57
  273.4 8.3 slice-start.8
  275.0 6.8 slice-start.9
  278.3 9.1 copy-start.27
  280.0 7.3 slice-start.20
  287.3 16.4 %copy-start.45 = (f32[384]{0:T(512)S(1)}, f32[384]{0:T(512)}, u32[]{:S(2)}) copy-start(f32[384]{0:T(512)} %copy-done.44) | copy-start | bytes 4612 | tf_op jit(solution)/shard_map/cond
  287.4 19.0 %copy-start.1 = (f32[384,768]{1,0:T(8,128)S(1)}, f32[384,768]{1,0:T(8,128)}, u32[]{:S(2)}) copy-start(f32[384,768]{1,0:T(8,128)} %copy-done) | copy-start | bytes 3538948 | tf_op jit(solution)/shard_map/cond
  307.5 8.4 copy-start.29
  307.5 8.4 copy-start.2
  308.6 7.3 copy-start.31
  309.2 5.5 collective-permute-start.1
  359.8 92.4 %collective-permute-start.2 = (bf16[18,384]{1,0:T(8,128)(2,1)S(1)}, bf16[18,384]{1,0:T(8,128)(2,1)S(1)}, u32[]{:S(2)}, u32[]{:S(2)}) collective-permute-start(bf16[18,384]{1,0:T(8,128)(2,1)S(1)} %fusion.315), channel_id=1, source_target_pairs={{16,0},{17,1},{18,2},{19,3},{20,4},{21,5},{22,6},{23,7},{24,8},{25... | collective-permute-start | bytes 41480 | tf_op jit(solution)/shard_map/ppermute | solution.py:22
  458.5 32.7 %copy-start.3 = (f32[384,768]{1,0:T(8,128)S(1)}, f32[384,768]{1,0:T(8,128)}, u32[]{:S(2)}) copy-start(f32[384,768]{1,0:T(8,128)} %copy-done.2) | copy-start | bytes 3538948
  461.6 14.5 %slice-start.26 = ((s8[4718592]{0:T(1024)(128)(4,1)}), s8[4194304]{0:T(1024)(128)(4,1)S(1)}, s32[]{:S(2)}) async-start(s8[4718592]{0:T(1024)(128)(4,1)} %bitcast.436), calls=%async_computation.48 | async-start | bytes 8388608 | tf_op jit(solution)/shard_map/cond
  463.9 12.2 slice-start.27
  463.9 18.3 %slice-start.14 = ((s8[4718592]{0:T(1024)(128)(4,1)}), s8[4194304]{0:T(1024)(128)(4,1)S(1)}, s32[]{:S(2)}) async-start(s8[4718592]{0:T(1024)(128)(4,1)} %bitcast.418), calls=%async_computation.36 | async-start | bytes 8388608 | tf_op jit(solution)/shard_map/cond
  491.2 53.3 %copy-start.9 = (f32[384,768]{1,0:T(8,128)S(1)}, f32[384,768]{1,0:T(8,128)}, u32[]{:S(2)}) copy-start(f32[384,768]{1,0:T(8,128)} %copy-done.8) | copy-start | bytes 3538948
  532.5 5.7 collective-permute-start.3
  544.5 37.5 %copy-start.7 = (f32[384,768]{1,0:T(8,128)S(1)}, f32[384,768]{1,0:T(8,128)}, u32[]{:S(2)}) copy-start(f32[384,768]{1,0:T(8,128)} %get-tuple-element.400) | copy-start | bytes 3538948
  544.5 37.5 %copy-start.11 = (bf16[1,768,768]{2,1,0:T(8,128)(2,1)S(1)}, bf16[1,768,768]{2,1,0:T(8,128)(2,1)}, u32[]{:S(2)}) copy-start(bf16[1,768,768]{2,1,0:T(8,128)(2,1)} %all-gather.7.cloned.1.call-done) | copy-start | bytes 3538948
  548.9 14.5 %slice-start.28 = ((s8[4718592]{0:T(1024)(128)(4,1)}), s8[4194304]{0:T(1024)(128)(4,1)S(1)}, s32[]{:S(2)}) async-start(s8[4718592]{0:T(1024)(128)(4,1)} %bitcast.438), calls=%async_computation.50 | async-start | bytes 8388608 | tf_op jit(solution)/shard_map/cond
  551.2 12.1 slice-start.29
  551.2 18.2 %slice-start.16 = ((s8[4718592]{0:T(1024)(128)(4,1)}), s8[4194304]{0:T(1024)(128)(4,1)S(1)}, s32[]{:S(2)}) async-start(s8[4718592]{0:T(1024)(128)(4,1)} %bitcast.420), calls=%async_computation.38 | async-start | bytes 8388608 | tf_op jit(solution)/shard_map/cond
  580.3 121.3 %reduce-scatter.32.cloned.1.call-start = ((), (), s32[]{:S(2)}) async-start(), calls=%async_computation.19 | async-start | bytes 417792
  582.0 38.4 %copy-start.55 = (f32[768]{0:T(1024)S(1)}, f32[768]{0:T(1024)}, u32[]{:S(2)}) copy-start(f32[768]{0:T(1024)} %copy-done.54) | copy-start | bytes 9220
  582.0 40.1 %copy-start.52 = (f32[768]{0:T(1024)S(1)}, f32[768]{0:T(1024)}, u32[]{:S(2)}) copy-start(f32[768]{0:T(1024)} %copy-done.51) | copy-start | bytes 9220
  620.4 129.9 %reduce-scatter.30.cloned.1.call-start = ((), (), s32[]{:S(2)}) async-start(), calls=%async_computation.18 | async-start | bytes 417792
  622.1 186.7 %reduce-scatter.28.cloned.1.call-start = ((), (), s32[]{:S(2)}) async-start(), calls=%async_computation.17 | async-start | bytes 417792
  623.8 243.1 %reduce-scatter.36.cloned.1.call-start = ((), (), s32[]{:S(2)}) async-start(), calls=%async_computation.21 | async-start | bytes 417792
  626.0 307.6 %reduce-scatter.22.cloned.1.call-start = ((), (), s32[]{:S(2)}) async-start(), calls=%async_computation.14 | async-start | bytes 2506752 | tf_op jit(solution)/shard_map/reduce_scatter | solution.py:420
  631.2 395.9 %reduce-scatter.20.cloned.1.call-start = ((), (), s32[]{:S(2)}) async-start(), calls=%async_computation.13 | async-start | bytes 7520256 | tf_op jit(solution)/shard_map/reduce_scatter | solution.py:419
  642.1 501.1 %reduce-scatter.26.cloned.1.call-start = ((), (), s32[]{:S(2)}) async-start(), calls=%async_computation.16 | async-start | bytes 10027008 | tf_op jit(solution)/shard_map/reduce_scatter | solution.py:413
  653.5 605.5 %reduce-scatter.24.cloned.1.call-start = ((), (), s32[]{:S(2)}) async-start(), calls=%async_computation.15 | async-start | bytes 10027008 | tf_op jit(solution)/shard_map/reduce_scatter | solution.py:412
  (44 other events, 129.6 us)
Sparse Core Ops, SparseCore 0:
  10.3 41.3 all-gather.6
  53.9 46.1 all-gather.4
  102.4 52.2 all-gather.8
  156.8 51.7 all-gather.10
  580.5 53.2 reduce-scatter.33
  637.5 54.6 reduce-scatter.31
  695.7 54.5 reduce-scatter.29
  754.2 54.5 reduce-scatter.27
  812.3 54.5 reduce-scatter.35
  871.6 61.9 reduce-scatter.21
  938.2 88.9 reduce-scatter.19
  1032.3 110.8 reduce-scatter.25
  1147.8 111.0 reduce-scatter.23
where the time goes:
time: 1270 us
  waiting for transfers between devices  780 us (61%)
  matrix products  196 us (15%)
  other arithmetic  92.5 us (7%)
  blocking collectives  85.1 us (7%)
  local copies, waits for them, and re-layouts  71 us (6%)
  loops' own time  16.9 us (1%)
  between operations  15.9 us (1%)
    unnamed x18, waiting for transfers between devices  164 us
    reduce_scatter x1, waiting for transfers between devices, on_device(): lax.psum_scatter(down_grad[None], 'dp', scatter_dimension=1, tiled=True)  116 us
    reduce_scatter x1, waiting for transfers between devices, on_device(): lax.psum_scatter(up_grad[None], 'dp', scatter_dimension=1, tiled=True)  116 us
    ppermute x4, waiting for transfers between devices, passed_along(): return lax.ppermute(array, axis, pairs)  94.4 us
    reduce_scatter x1, waiting for transfers between devices, on_device(): lax.psum_scatter(qkv_grad[None], 'dp', scatter_dimension=1, tiled=True)  93.6 us
    reduce_scatter x1, waiting for transfers between devices, on_device(): lax.psum_scatter(out_grad[None], 'dp', scatter_dimension=1, tiled=True)  65.3 us
    all_gather x1, waiting for transfers between devices, on_device(): lax.all_gather(up_weight, 'dp', axis=1, tiled=True)  54.6 us
    all_gather x1, waiting for transfers between devices, on_device(): lax.all_gather(down_weight, 'dp', axis=1, tiled=True)  54 us
  transfers between devices with their start and end apart: 17, of which 14 were waited for; matrix products, arithmetic and copies ran while one was open for 9% of the time, Pallas kernels for 0%

commit v1 on v0

--- a/solution.py
+++ b/solution.py
@@ -4,6 +4,8 @@
 import jax
 import jax.numpy as jnp
 from jax import lax
+from jax.experimental import pallas as pl
+from jax.experimental.pallas import tpu as pltpu
 from jax.sharding import PartitionSpec as P
 
 HEADS = 12
@@ -235,6 +237,371 @@
 
 def join_rows(pieces):
     return jax.tree.map(lambda *members: jnp.concatenate(members, 0), *pieces)
+
+
+MESH_ID = pl.DeviceIdType.MESH
+
+
+def ring_place():
+    seg = lax.axis_index("segment")
+    here = lax.axis_index("dp")
+    core = lax.rem(here, 2)
+    col = lax.rem(here // 2, 2)
+    row = here // 4
+    return seg, here, core, col, row
+
+
+def meet_neighbours(seg, here, core, col, row, rows):
+    barrier = pltpu.get_barrier_semaphore()
+
+    def greet(other):
+        pl.semaphore_signal(barrier, inc=1, device_id=(seg, other), device_id_type=MESH_ID)
+
+    greet(here + 1 - 2 * core)
+    greet(here + 2 - 4 * col)
+
+    @pl.when(row > 0)
+    def _():
+        greet(here - 4)
+
+    @pl.when(row < rows - 1)
+    def _():
+        greet(here + 4)
+
+    has_two = jnp.logical_and(row > 0, row < rows - 1)
+    pl.semaphore_wait(barrier, jnp.where(has_two, 4, 3))
+
+
+def gather_body(rows, *refs):
+    n_arr = 3
+    shards = refs[:n_arr]
+    fulls = refs[n_arr : 2 * n_arr]
+    own_sem, send_sem, recv_sem = refs[2 * n_arr :]
+    seg, here, core, col, row = ring_place()
+    sib = here + 1 - 2 * core
+    xn = here + 2 - 4 * col
+
+    def block(arr, src):
+        height = shards[arr].shape[0]
+        return fulls[arr].at[pl.ds(pl.multiple_of(src * height, height), height)]
+
+    def copy(arr, src, first, slot, to):
+        return pltpu.make_async_remote_copy(
+            src_ref=shards[arr] if first else block(arr, src),
+            dst_ref=block(arr, src),
+            send_sem=send_sem.at[arr, slot],
+            recv_sem=recv_sem.at[arr, src],
+            device_id=(seg, to),
+            device_id_type=MESH_ID,
+        )
+
+    def arrive(arr, src):
+        copy(arr, src, False, 0, sib).wait_recv()
+
+    def index(src_row, src_col):
+        return (src_row * 2 + src_col) * 2 + core
+
+    def to_sib(arr, src_row, src_col, first=False):
+        return copy(arr, index(src_row, src_col), first, 3 * rows + src_row * 2 + src_col, sib)
+
+    def to_x(arr, src_row, first=False):
+        return copy(arr, index(src_row, col), first, 2 * rows + src_row, xn)
+
+    def to_up(arr, src_row, first=False):
+        return copy(arr, index(src_row, col), first, src_row, here + 4)
+
+    def to_down(arr, src_row, first=False):
+        return copy(arr, index(src_row, col), first, rows + src_row, here - 4)
+
+    def own_copy(arr):
+        return pltpu.make_async_copy(shards[arr], block(arr, here), own_sem.at[arr])
+
+    def own(arr):
+        @pl.when(row < rows - 1)
+        def _():
+            to_up(arr, row, True).start()
+
+        @pl.when(row > 0)
+        def _():
+            to_down(arr, row, True).start()
+
+        to_x(arr, row, True).start()
+        to_sib(arr, row, col, True).start()
+        own_copy(arr).start()
+
+    def away(arr, dist):
+        @pl.when(row - dist >= 0)
+        def _():
+            src_row = row - dist
+            arrive(arr, index(src_row, col))
+
+            @pl.when(row < rows - 1)
+            def _():
+                to_up(arr, src_row).start()
+
+            to_x(arr, src_row).start()
+            to_sib(arr, src_row, col).start()
+
+        @pl.when(row + dist < rows)
+        def _():
+            src_row = row + dist
+            arrive(arr, index(src_row, col))
+
+            @pl.when(row > 0)
+            def _():
+                to_down(arr, src_row).start()
+
+            to_x(arr, src_row).start()
+            to_sib(arr, src_row, col).start()
+
+    def across(arr):
+        def at(src_row):
+            arrive(arr, index(src_row, 1 - col))
+            to_sib(arr, src_row, 1 - col).start()
+
+        at(row)
+        for dist in range(1, rows):
+            pl.when(row - dist >= 0)(lambda: at(row - dist))
+            pl.when(row + dist < rows)(lambda: at(row + dist))
+
+    meet_neighbours(seg, here, core, col, row, rows)
+    for arr in range(n_arr):
+        own(arr)
+        if arr > 0:
+            away(arr - 1, rows - 1)
+        away(arr, 1)
+        if arr > 0:
+            across(arr - 1)
+        for dist in range(2, rows - 1):
+            away(arr, dist)
+    away(n_arr - 1, rows - 1)
+    across(n_arr - 1)
+    for arr in range(n_arr):
+        own_copy(arr).wait()
+
+        @pl.loop(0, 2 * rows)
+        def _(i):
+            copy(arr, 2 * i + 1 - core, False, 0, sib).wait_recv()
+            copy(arr, 2 * i + core, False, 3 * rows + i, sib).wait_send()
+
+        @pl.loop(0, rows)
+        def _(i):
+            to_x(arr, i).wait_send()
+
+            @pl.when(jnp.logical_and(i <= row, row < rows - 1))
+            def _():
+                to_up(arr, i).wait_send()
+
+            @pl.when(jnp.logical_and(i >= row, row > 0))
+            def _():
+                to_down(arr, i).wait_send()
+
+
+def gather_blocks(shards):
+    count = lax.axis_size("dp")
+    rows = count // 4
+    any_spec = pl.BlockSpec(memory_space=pl.ANY)
+    return pl.pallas_call(
+        partial(gather_body, rows),
+        out_shape=tuple(
+            jax.ShapeDtypeStruct((count * s.shape[0], s.shape[1]), s.dtype) for s in shards
+        ),
+        in_specs=[any_spec] * 3,
+        out_specs=(any_spec,) * 3,
+        scratch_shapes=[
+            pltpu.SemaphoreType.DMA((3,)),
+            pltpu.SemaphoreType.DMA((3, 5 * rows)),
+            pltpu.SemaphoreType.DMA((3, 4 * rows)),
+        ],
+        compiler_params=pltpu.CompilerParams(collective_id=1, has_side_effects=True),
+        name="gather_weights",
+    )(*shards)
+
+
+def scatter_body(rows, *refs):
+    n_arr = 3
+    parts = refs[:n_arr]
+    outs = refs[n_arr : 2 * n_arr]
+    own, sibs, xsend, xrecv, zsend, zrecv = [
+        refs[(2 + i) * n_arr : (3 + i) * n_arr] for i in range(6)
+    ]
+    own_sem, sib_ssem, sib_rsem, x_ssem, x_rsem, z_ssem, z_rsem = refs[8 * n_arr :]
+    seg, here, core, col, row = ring_place()
+    sib = here + 1 - 2 * core
+    xn = here + 2 - 4 * col
+
+    def block(arr, dst):
+        height = outs[arr].shape[0]
+        return parts[arr].at[pl.ds(pl.multiple_of(dst * height, height), height)]
+
+    def remote(src, dst, ssem, rsem, to):
+        return pltpu.make_async_remote_copy(
+            src_ref=src,
+            dst_ref=dst,
+            send_sem=ssem,
+            recv_sem=rsem,
+            device_id=(seg, to),
+            device_id_type=MESH_ID,
+        )
+
+    def own_copy(arr, place):
+        return pltpu.make_async_copy(
+            block(arr, 2 * place + core), own[arr].at[place], own_sem.at[arr, place]
+        )
+
+    def sib_copy(arr, place):
+        return remote(
+            block(arr, 2 * place + 1 - core),
+            sibs[arr].at[place],
+            sib_ssem.at[arr, place],
+            sib_rsem.at[arr, place],
+            sib,
+        )
+
+    def x_copy(arr, dst_row):
+        return remote(
+            xsend[arr].at[dst_row],
+            xrecv[arr].at[dst_row],
+            x_ssem.at[arr, dst_row],
+            x_rsem.at[arr, dst_row],
+            xn,
+        )
+
+    def z_copy(arr, way, dst_row):
+        return remote(
+            zsend[arr].at[dst_row],
+            zrecv[arr].at[way, dst_row],
+            z_ssem.at[arr, dst_row],
+            z_rsem.at[arr, way, dst_row],
+            here + 4 - 8 * way,
+        )
+
+    def each_far(body):
+        @pl.loop(0, 2 * (rows - 1))
+        def _(i):
+            way = lax.rem(i, 2)
+            dst_row = row + (1 - 2 * way) * (rows - 1 - i // 2)
+            pl.when(jnp.logical_and(dst_row >= 0, dst_row < rows))(lambda: body(way, dst_row))
+
+    def start_pairs(arr):
+        def go(dst_row, at_col):
+            sib_copy(arr, 2 * dst_row + at_col).start()
+            own_copy(arr, 2 * dst_row + at_col).start()
+
+        each_far(lambda way, dst_row: go(dst_row, 1 - col))
+        go(row, 1 - col)
+        each_far(lambda way, dst_row: go(dst_row, col))
+        go(row, col)
+
+    def pair_sum(arr, place):
+        sib_copy(arr, place).wait_recv()
+        own_copy(arr, place).wait()
+        return own[arr][place].astype(jnp.float32) + sibs[arr][place].astype(jnp.float32)
+
+    def x_stage(arr):
+        def go(dst_row):
+            xsend[arr][dst_row] = pair_sum(arr, 2 * dst_row + 1 - col).astype(jnp.bfloat16)
+            x_copy(arr, dst_row).start()
+
+        each_far(lambda way, dst_row: go(dst_row))
+        go(row)
+
+    def column_sum(arr, dst_row):
+        x_copy(arr, dst_row).wait_recv()
+        return pair_sum(arr, 2 * dst_row + col) + xrecv[arr][dst_row].astype(jnp.float32)
+
+    def z_stage(arr):
+        def go(way, dst_row):
+            behind = row - 1 + 2 * way
+
+            @pl.when(jnp.logical_and(behind >= 0, behind < rows))
+            def _():
+                z_copy(arr, way, dst_row).wait_recv()
+
+            total = column_sum(arr, dst_row) + zrecv[arr][way, dst_row].astype(jnp.float32)
+            zsend[arr][dst_row] = total.astype(jnp.bfloat16)
+            z_copy(arr, way, dst_row).start()
+
+        each_far(go)
+
+        @pl.when(row > 0)
+        def _():
+            z_copy(arr, 0, row).wait_recv()
+
+        @pl.when(row < rows - 1)
+        def _():
+            z_copy(arr, 1, row).wait_recv()
+
+        outs[arr][...] = (
+            column_sum(arr, row)
+            + zrecv[arr][0, row].astype(jnp.float32)
+            + zrecv[arr][1, row].astype(jnp.float32)
+        )
+
+    meet_neighbours(seg, here, core, col, row, rows)
+    for arr in range(n_arr):
+        start_pairs(arr)
+
+    def clear(way):
+        for arr in range(n_arr):
+            zrecv[arr][way] = jnp.zeros(zrecv[arr].shape[1:], jnp.bfloat16)
+
+    pl.when(row == 0)(lambda: clear(0))
+    pl.when(row == rows - 1)(lambda: clear(1))
+    x_stage(0)
+    for arr in range(n_arr):
+        if arr + 1 < n_arr:
+            x_stage(arr + 1)
+        z_stage(arr)
+    for arr in range(n_arr):
+
+        @pl.loop(0, 2 * rows)
+        def _(i):
+            sib_copy(arr, i).wait_send()
+
+        @pl.loop(0, rows)
+        def _(i):
+            x_copy(arr, i).wait_send()
+
+        each_far(lambda way, dst_row: z_copy(arr, way, dst_row).wait_send())
+
+
+def scatter_sums(parts):
+    count = lax.axis_size("dp")
+    rows = count // 4
+    any_spec = pl.BlockSpec(memory_space=pl.ANY)
+    vmem_spec = pl.BlockSpec(memory_space=pltpu.VMEM)
+    shapes = [(p.shape[0] // count, p.shape[1]) for p in parts]
+
+    def buffers(*lead):
+        return [pltpu.VMEM(lead + s, jnp.bfloat16) for s in shapes]
+
+    dma = pltpu.SemaphoreType.DMA
+    return pl.pallas_call(
+        partial(scatter_body, rows),
+        out_shape=tuple(jax.ShapeDtypeStruct(s, jnp.float32) for s in shapes),
+        in_specs=[any_spec] * 3,
+        out_specs=(vmem_spec,) * 3,
+        scratch_shapes=buffers(2 * rows)
+        + buffers(2 * rows)
+        + buffers(rows)
+        + buffers(rows)
+        + buffers(rows)
+        + buffers(2, rows)
+        + [
+            dma((3, 2 * rows)),
+            dma((3, 2 * rows)),
+            dma((3, 2 * rows)),
+            dma((3, rows)),
+            dma((3, rows)),
+            dma((3, rows)),
+            dma((3, 2, rows)),
+        ],
+        compiler_params=pltpu.CompilerParams(
+            collective_id=2, has_side_effects=True, vmem_limit_bytes=56 << 20
+        ),
+        name="scatter_sums",
+    )(*parts)
 
 
 def on_device(
@@ -260,21 +627,33 @@
     row_total = per_micro * patches
     validity = extent_mask(image_extent, patches)
     own_input = segment_input[0]
-    attn_set = (
-        lax.all_gather(norm1_gain, "dp", axis=1, tiled=True),
-        lax.all_gather(norm1_bias, "dp", axis=1, tiled=True),
-        lax.all_gather(qkv_weight, "dp", axis=1, tiled=True),
-        lax.all_gather(out_weight, "dp", axis=1, tiled=True),
-        lax.all_gather(code_maps, "dp", axis=1, tiled=True),
-    )
-    attn_weights = tuple((member[0] for member in attn_set))
-    mlp_set = (
-        lax.all_gather(norm2_gain, "dp", axis=1, tiled=True),
-        lax.all_gather(norm2_bias, "dp", axis=1, tiled=True),
-        lax.all_gather(up_weight, "dp", axis=1, tiled=True),
-        lax.all_gather(down_weight, "dp", axis=1, tiled=True),
-    )
-    mlp_weights = tuple((member[0] for member in mlp_set))
+    qkv_width = qkv_weight.shape[2]
+    small = jnp.concatenate(
+        [code_maps[0]]
+        + [v[0][:, None] for v in (norm1_gain, norm1_bias, norm2_gain, norm2_bias)],
+        axis=1,
+    )
+    small = jnp.pad(small, ((0, 0), (0, 128 - small.shape[1])))
+    shards = (
+        jnp.concatenate([qkv_weight[0], out_weight[0], small], axis=1),
+        up_weight[0],
+        down_weight[0],
+    )
+    by_kernel = shards[0].shape[0] % 16 == 0
+    if by_kernel:
+        attn_all, up_all, down_all = gather_blocks(shards)
+    else:
+        attn_all, up_all, down_all = [lax.all_gather(s, "dp", axis=0, tiled=True) for s in shards]
+    small_all = attn_all[:, qkv_width + features :]
+    norms = small_all[:, CODE_BITS : CODE_BITS + 4].T
+    attn_weights = (
+        norms[0],
+        norms[1],
+        attn_all[:, :qkv_width],
+        attn_all[:, qkv_width : qkv_width + features],
+        small_all[:, :CODE_BITS],
+    )
+    mlp_weights = (norms[2], norms[3], up_all, down_all)
     code_in = jnp.zeros((CODE_BITS, row_total), jnp.bfloat16)
     code_grad = jnp.zeros((CODE_BITS, row_total), jnp.bfloat16)
     energies = jnp.zeros((3,), jnp.float32)
@@ -322,19 +701,6 @@
         decoded.append(record_item[3])
     weight_pair = (attn_weights, mlp_weights)
     attn_use, mlp_use = weight_pair
-    mlp_shards = (
-        jnp.zeros(norm2_gain.shape, jnp.float32),
-        jnp.zeros(norm2_bias.shape, jnp.float32),
-        jnp.zeros(up_weight.shape, jnp.float32),
-        jnp.zeros(down_weight.shape, jnp.float32),
-    )
-    attn_shards = (
-        jnp.zeros(norm1_gain.shape, jnp.float32),
-        jnp.zeros(norm1_bias.shape, jnp.float32),
-        jnp.zeros(qkv_weight.shape, jnp.float32),
-        jnp.zeros(out_weight.shape, jnp.float32),
-        jnp.zeros(code_maps.shape, jnp.float32),
-    )
     small_total = (
         jnp.zeros((features,), jnp.float32),
         jnp.zeros((features,), jnp.float32),
@@ -342,12 +708,12 @@
         jnp.zeros((features,), jnp.float32),
         jnp.zeros(attn_use[4].shape, jnp.float32),
     )
-    sums = (mlp_shards, attn_shards, small_total, [], [])
+    sums = (small_total, [], [])
     results = []
     for step_index in range(microbatch_count + 1):
         position = microbatch_count - step_index - segment_no
         run_attn_use, run_mlp_use = weight_pair
-        run_mlp_shards, run_attn_shards, run_small_total, mlp_pieces, attn_pieces = sums
+        run_small_total, mlp_pieces, attn_pieces = sums
         code_maps_all = run_attn_use[4]
         saved_tensor, applied_code, patch_keep_mask, block_result = saved_tensors[
             microbatch_count - step_index
@@ -404,26 +770,10 @@
             run_small_total,
             (mlp_small[0], mlp_small[1], attn_small[0], attn_small[1], map_part),
         )
-        if step_index == microbatch_count:
-            up_grad, down_grad = mlp_weight_grads(join_rows(mlp_pieces))
-            run_mlp_shards = (
-                lax.psum_scatter(run_small_total[0][None], "dp", scatter_dimension=1, tiled=True),
-                lax.psum_scatter(run_small_total[1][None], "dp", scatter_dimension=1, tiled=True),
-                lax.psum_scatter(up_grad[None], "dp", scatter_dimension=1, tiled=True),
-                lax.psum_scatter(down_grad[None], "dp", scatter_dimension=1, tiled=True),
-            )
-            qkv_grad, out_grad = attention_weight_grads(join_rows(attn_pieces))
-            run_attn_shards = (
-                lax.psum_scatter(run_small_total[2][None], "dp", scatter_dimension=1, tiled=True),
-                lax.psum_scatter(run_small_total[3][None], "dp", scatter_dimension=1, tiled=True),
-                lax.psum_scatter(qkv_grad[None], "dp", scatter_dimension=1, tiled=True),
-                lax.psum_scatter(out_grad[None], "dp", scatter_dimension=1, tiled=True),
-                lax.psum_scatter(run_small_total[4][None], "dp", scatter_dimension=1, tiled=True),
-            )
         grad_in, code_grad, sums = (
             grad_in,
             code_next,
-            (run_mlp_shards, run_attn_shards, run_small_total, mlp_pieces, attn_pieces),
+            (run_small_total, mlp_pieces, attn_pieces),
         )
         results.append(grad_in)
     for micro_index in range(microbatch_count):
@@ -431,22 +781,41 @@
             is_first, results[microbatch_count - micro_index], decoded[micro_index + 1]
         )
         pieces.append(chosen.reshape(per_micro, patches, features))
-    mlp_shards, attn_shards = (sums[0], sums[1])
+    small_total, mlp_pieces, attn_pieces = sums
+    up_grad, down_grad = mlp_weight_grads(join_rows(mlp_pieces))
+    qkv_grad, out_grad = attention_weight_grads(join_rows(attn_pieces))
+    small_grad = jnp.concatenate(
+        [small_total[4]]
+        + [small_total[i][:, None] for i in (2, 3, 0, 1)],
+        axis=1,
+    )
+    small_grad = jnp.pad(small_grad, ((0, 0), (0, 128 - small_grad.shape[1])))
+    attn_grad = jnp.concatenate([qkv_grad, out_grad, small_grad], axis=1)
+    if by_kernel:
+        low_parts = tuple(v.astype(jnp.bfloat16) for v in (down_grad, up_grad, attn_grad))
+        down_shard, up_shard, attn_shard = scatter_sums(low_parts)
+    else:
+        down_shard, up_shard, attn_shard = [
+            lax.psum_scatter(v, "dp", scatter_dimension=0, tiled=True)
+            for v in (down_grad, up_grad, attn_grad)
+        ]
+    small_shard = attn_shard[:, qkv_width + features :]
+    norm_shards = [small_shard[:, CODE_BITS + i][None] for i in range(4)]
     segment_output = jnp.concatenate(pieces, 0)[None]
     energy_all, valid_all = lax.psum((energies, jnp.sum(validity)), "dp")
     rms_stats = jnp.sqrt(energy_all / (valid_all * features))[None]
     return (
         segment_output,
         rms_stats,
-        attn_shards[0],
-        attn_shards[1],
-        mlp_shards[0],
-        mlp_shards[1],
-        attn_shards[2],
-        attn_shards[3],
-        mlp_shards[2],
-        mlp_shards[3],
-        attn_shards[4],
+        norm_shards[0],
+        norm_shards[1],
+        norm_shards[2],
+        norm_shards[3],
+        attn_shard[:, :qkv_width][None],
+        attn_shard[:, qkv_width : qkv_width + features][None],
+        up_shard[None],
+        down_shard[None],
+        small_shard[:, :CODE_BITS][None],
     )
 
 

time: 1270 us -> 688 us (0.54)
  waiting for transfers between devices: 780 us -> 94 us
  Pallas kernels: 0 us -> 176 us
  blocking collectives: 85.1 us -> 30.1 us
  between operations: 15.9 us -> 2.11 us
    reduce_scatter x4 -> x0, waiting for transfers between devices: 391 us -> none  [the longest x1 116 us: on_device(): lax.psum_scatter(down_grad[None], 'dp', scatter_dimension=1, tiled=True)]
    pallas_call x0 -> x2, Pallas kernels: none -> 176 us  [the longest x1 88.9 us: scatter_sums(): pl.pallas_call(partial(scatter_body, rows), out_shape=tuple((jax.ShapeDty...]
    unnamed x18 -> x0, waiting for transfers between devices: 164 us -> none
    all_gather x4 -> x0, waiting for transfers between devices: 130 us -> none  [the longest x1 54.6 us: on_device(): lax.all_gather(up_weight, 'dp', axis=1, tiled=True)]
    squeeze x1 -> x0, blocking collectives: 30.6 us -> none  [on_device(): attn_weights = tuple((member[0] for member in attn_set))]
    all_gather x1 -> x0, blocking collectives: 24.3 us -> none  [on_device(): lax.all_gather(code_maps, 'dp', axis=1, tiled=True)]
    unnamed x80, local copies, waits for them, and re-layouts: 23.1 us -> 8.26 us
    another operation x27 -> x31, local copies, waits for them, and re-layouts: 33.6 us -> 34.9 us
  transfers between devices with their start and end apart: 17 -> 4, of which waited for: 14 -> 4; matrix products, arithmetic and copies ran while one was open for 9% -> 1% of each run, Pallas kernels for 0% -> 0%
where the time goes in v1:
time: 688 us; the launch traced here: 682 us
  matrix products  192 us (28%)
  Pallas kernels  176 us (26%)
  other arithmetic  98.7 us (14%)
  waiting for transfers between devices  94 us (14%)
  local copies, waits for them, and re-layouts  69.6 us (10%)
  blocking collectives  30.1 us (4%)
  loops' own time  10.8 us (2%)
  starting transfers between devices  8.06 us (1%)
    ppermute x4, waiting for transfers between devices, passed_along(): return lax.ppermute(array, axis, pairs)  94 us
    pallas_call x1, Pallas kernels, scatter_sums(): pl.pallas_call(partial(scatter_body, rows), out_shape=tuple((jax.ShapeDty...  88.9 us
    pallas_call x1, Pallas kernels, gather_blocks(): pl.pallas_call(partial(gather_body, rows), out_shape=tuple((jax.ShapeDtyp...  87.5 us
    another operation x27, local copies, waits for them, and re-layouts  31.9 us
    psum x1, blocking collectives, on_device(): energy_all, valid_all = lax.psum((energies, jnp.sum(validity)), 'dp')  30.1 us
    dot_general x2, matrix products, mlp_forward(): jnp.dot(activation, w_down, preferred_element_type=jnp.float32)  29.8 us
    convert_element_type x2, other arithmetic, mlp_backward(): activation.astype(jnp.bfloat16)  24.3 us
    dot_general x4, matrix products, masked_scores(): jnp.einsum('iqhe,ikhe->ihqk', queries, key_rows, preferred_element_type=j...  16.8 us
  transfers between devices with their start and end apart: 4, of which 4 were waited for; matrix products, arithmetic and copies ran while one was open for 1% of the time, Pallas kernels for 0%

profile of v1, /device:TPU:0, one launch (start us, length us, event | category | flops | bytes accessed | tf_op | source)
XLA Modules:
  0.0 681.8 jit_solution(2220678376195376324)
XLA Ops:
  6.3 87.5 %gather_weights.1 = (bf16[768,3200]{1,0:T(8,128)(2,1)}, bf16[768,3072]{1,0:T(8,128)(2,1)}, bf16[3072,768]{1,0:T(8,128)(2,1)}) custom-call(bf16[48,3200]{1,0:T(8,128)(2,1)} %fusion.323.refs_0_, bf16[48,3072]{1,0:T(8,128)(2,1)} %bitcast.332, bf16[192,768]{1,0:T(8,128)(2,1)} %bitcast.333), custom_call_target="tpu_custom_call" | custom-call | tf_op jit(solution)/shard_map/gather_weights/pallas_call | solution.py:404
  94.9 4.1 slice.124
  107.5 46.1 %conditional.9 = (f32[384,768]{1,0:T(8,128)}, bf16[384,2304]{1,0:T(8,128)(2,1)}, f32[1,12,384]{2,1,0:T(8,128)S(1)}, bf16[384,768]{0,1:T(8,128)(2,1)}, f32[384,76...) conditional(s32[]{:T(128)} %convert_element_type.377, () %tuple.91, ...), branch_computations={%region_0.1_spmd, %region_1.14_spmd} | conditional | flops 5996151296 | bytes 112885528 | solution.py:678
  110.2 2.9 convolution_convert_fusion
  113.1 3.9 copy.116
  117.0 3.1 fusion.24
  121.7 4.0 fusion.39
  125.7 2.8 fusion.367
  130.3 5.6 fusion.40
  135.9 14.9 %multiply_reduce_fusion.11 = (f32[384]{0:T(512)S(1)}, f32[384]{0:T(512)S(1)}, bf16[384,768]{1,0:T(8,128)(2,1)}) fusion(f32[384,768]{1,0:T(8,128)} %get-tuple-element.804, bf16[3072,768]{1,0:T(8,128)(2,1)S(1)} %bitcast.367, f32[384,3072]{1,0:T(8,128)} %fusion.40), kind=kOutput, calls=%fused_computation.120 | convolution fusion | flops 1890385152 | bytes 11209728 | tf_op jit(solution)/shard_map/cond/branch_1_fun/dot_general | solution.py:94
  161.0 47.1 %conditional.10 = (f32[384,768]{1,0:T(8,128)}, f32[384,768]{1,0:T(8,128)S(1)}, bf16[384,2304]{1,0:T(8,128)(2,1)}, f32[1,12,384]{2,1,0:T(8,128)S(1)}, bf16[384,76...) conditional(s32[]{:T(128)} %convert_element_type.381, () %tuple.95, ...), branch_computations={%region_15.16_spmd, %region_16.29_spmd} | conditional | flops 5996151296 | bytes 119975808 | solution.py:678
  163.4 3.0 convolution_convert_fusion.1
  166.3 3.9 copy.119
  170.2 3.1 fusion.82
  174.9 4.0 fusion.97
  183.5 5.6 fusion.98
  189.0 14.9 %fusion.369 = (bf16[384,768]{1,0:T(8,128)(2,1)}, f32[384,768]{1,0:T(8,128)}, f32[384]{0:T(512)S(1)}) fusion(f32[384,768]{1,0:T(8,128)} %get-tuple-element.822, bf16[3072,768]{1,0:T(8,128)(2,1)S(1)} %bitcast.369, f32[384,3072]{1,0:T(8,128)} %fusion.98), kind=kOutput, calls=%fused_computation.637 | convolution fusion | flops 1889795712 | bytes 12387840 | tf_op jit(solution)/shard_map/cond/branch_1_fun/dot_general | solution.py:94
  211.8 4.2 collective-permute-start.1
  218.7 7.5 %conditional.11 = (f32[384,768]{1,0:T(8,128)}, f32[384,768]{1,0:T(8,128)S(1)}, bf16[384,2304]{1,0:T(8,128)(2,1)}, f32[1,12,384]{2,1,0:T(8,128)S(1)}, bf16[384,76...) conditional(s32[]{:T(128)} %convert_element_type.385, () %tuple.99, ...), branch_computations={%region_30.31_spmd, %region_31.44_spmd} | conditional | flops 5996151296 | bytes 122322784 | solution.py:678
  229.7 7.4 %conditional.12 = (f32[384,768]{1,0:T(8,128)}, f32[768]{0:T(1024)}, f32[768]{0:T(1024)}, bf16[384,3072]{1,0:T(8,128)(2,1)}, bf16[384,768]{1,0:T(8,128)(2,1)}, /*...) conditional(s32[]{:T(128)} %convert_element_type.385, () %tuple.101, (pred[]{:T(512)}, ...), branch_computations={%region_46.47_spmd, %region_47.54_spmd} | conditional | flops 3725036288 | bytes 95017200 | solution.py:740
  237.1 14.8 %conditional.13 = (f32[768]{0:T(1024)}, f32[768]{0:T(1024)}, bf16[384,768]{1,0:T(8,128)(2,1)}, bf16[384,768]{1,0:T(8,128)(2,1)}, bf16[384,768]{1,0:T(8,128)(2,1)...) conditional(s32[]{:T(128)} %convert_element_type.385, () %tuple.98, (f32[384,768]{1,0:T(8,128)S(1)}, ...), branch_computations={%region_54.55_spmd, %region_55.63_spmd} | conditional | flops 2982443264 | bytes 120554688 | solution.py:744
  256.6 30.1 %all-reduce.2 = (f32[3]{0:T(128)S(1)}, f32[]{:T(128)}) all-reduce(f32[3]{0:T(128)S(1)} %add_add_fusion.14, f32[]{:T(128)} %get-tuple-element.738), channel_id=1, replica_groups=mesh['segment'=2,'dp'=16] {'dp'}, use_global_device_ids=true, to_apply=%region_99.100 | all-reduce | flops 4 | bytes 32 | tf_op jit(solution)/shard_map/psum | solution.py:805
  289.8 62.6 %collective-permute-done.2 = bf16[18,384]{1,0:T(8,128)(2,1)S(1)} collective-permute-done((bf16[18,384]{1,0:T(8,128)(2,1)S(1)}, bf16[18,384]{1,0:T(8,128)(2,1)S(1)}, u32[]{:S(2)}, u32[]{:S(2)}) %collective-permute-start.2) | collective-permute-done | bytes 13856 | tf_op jit(solution)/shard_map/ppermute | solution.py:24
  357.1 34.0 %conditional.14 = (f32[384,768]{1,0:T(8,128)}, f32[768]{0:T(1024)}, f32[768]{0:T(1024)}, bf16[384,3072]{1,0:T(8,128)(2,1)}, bf16[384,768]{1,0:T(8,128)(2,1)}, /*...) conditional(s32[]{:T(128)} %convert_element_type.381, () %tuple.97, (pred[]{:T(512)}, f32[384,768]{1,0:T(8,128)}, ...), branch_computations={%region_64.65_spmd, %region_65.72_spmd} | conditional | flops 3725036288 | bytes 85579952 | solution.py:740
  363.8 12.1 %multiply_convert_fusion.1 = (bf16[384,3072]{1,0:T(8,128)(2,1)}, f32[384,3072]{1,0:T(8,128)S(1)}) fusion(f32[384,3072]{1,0:T(8,128)} %get-tuple-element.261), kind=kLoop, calls=%fused_computation.32 | loop fusion | flops 76677120 | bytes 11796480 | tf_op jit(solution)/shard_map/cond/branch_1_fun/convert_element_type | solution.py:138
  375.9 6.1 add_convert_fusion.2
  382.1 4.9 multiply_reduce_fusion.3
  391.0 39.6 %conditional.15 = (f32[384,768]{1,0:T(8,128)}, f32[768]{0:T(1024)}, f32[768]{0:T(1024)}, bf16[384,768]{1,0:T(8,128)(2,1)}, bf16[384,768]{1,0:T(8,128)(2,1)}, /*i...) conditional(s32[]{:T(128)} %convert_element_type.381, () %tuple.94, ...), branch_computations={%region_72.73_spmd, %region_73.81_spmd} | conditional | flops 2982443264 | bytes 119375016 | solution.py:744
  391.0 3.9 copy.143
  394.9 5.2 fusion.232
  405.0 6.0 multiply_reduce_fusion.37
  419.3 5.0 multiply_reduce_fusion.38
  439.1 28.5 %collective-permute-done.3 = bf16[18,384]{1,0:T(8,128)(2,1)S(1)} collective-permute-done((bf16[18,384]{1,0:T(8,128)(2,1)S(1)}, bf16[18,384]{1,0:T(8,128)(2,1)S(1)}, u32[]{:S(2)}, u32[]{:S(2)}) %collective-permute-start.3) | collective-permute-done | bytes 13856 | tf_op jit(solution)/shard_map/ppermute | solution.py:24
  470.2 34.2 %conditional.16 = (f32[384,768]{1,0:T(8,128)}, f32[768]{0:T(1024)}, f32[768]{0:T(1024)}, bf16[384,3072]{1,0:T(8,128)(2,1)}, bf16[384,768]{1,0:T(8,128)(2,1)}, /*...) conditional(s32[]{:T(128)} %convert_element_type.377, () %tuple.93, (pred[]{:T(512)}, f32[384,768]{1,0:T(8,128)}, ...), branch_computations={%region_82.83_spmd, %region_83.90_spmd} | conditional | flops 3725036288 | bytes 85579952 | solution.py:740
  476.9 12.1 %multiply_convert_fusion.2 = (bf16[384,3072]{1,0:T(8,128)(2,1)}, f32[384,3072]{1,0:T(8,128)S(1)}) fusion(f32[384,3072]{1,0:T(8,128)} %get-tuple-element.280), kind=kLoop, calls=%fused_computation.62 | loop fusion | flops 76677120 | bytes 11796480 | tf_op jit(solution)/shard_map/cond/branch_1_fun/convert_element_type | solution.py:138
  489.0 6.2 add_convert_fusion.4
  495.2 4.9 multiply_reduce_fusion.6
  506.3 37.0 %conditional.17 = (f32[384,768]{1,0:T(8,128)S(1)}, f32[768]{0:T(1024)S(1)}, f32[768]{0:T(1024)S(1)}, bf16[384,768]{1,0:T(8,128)(2,1)S(1)}, bf16[384,768]{1,0:T(8...) conditional(s32[]{:T(128)} %convert_element_type.377, () %tuple.90, (f32[1,384]{1,0:T(1,128)}, ...), branch_computations={%region_90.91_spmd, %region_91.99_spmd} | conditional | flops 2982148352 | bytes 118785216 | solution.py:744
  506.3 3.9 copy.145
  510.1 5.3 fusion.251
  519.7 6.1 multiply_reduce_fusion.41
  534.2 4.4 multiply_reduce_fusion.42
  547.3 7.9 %fusion.274 = bf16[768,2304]{1,0:T(8,128)(2,1)S(1)} fusion(bf16[384,2304]{0,1:T(8,128)(2,1)} %get-tuple-element.435, bf16[384,2304]{0,1:T(8,128)(2,1)} %get-tuple-element.434, bf16[384,2304]{0,1:T(8,128)(2,1)} %get-tuple-element.433, bf16[384,768]{1,0:T(8,128)(2,1)} %get-tuple-element.432, bf16[384,768]{1,0:T(8,128)(2,1)} %get-tuple-element.431, ...), kind=kOutput, calls=%fused_computation.489 | convolution fusion | flops 4099866624 | bytes 10616832 | tf_op jit(solution)/shard_map/rd,re->de/dot_general | solution.py:233
  555.2 3.7 fusion.310
  558.9 2.8 fusion.283.refs_2_
  561.8 10.5 %fusion.280.refs_1_ = bf16[768,3072]{1,0:T(8,128)(2,1)} fusion(bf16[384,3072]{1,0:T(8,128)(2,1)} %get-tuple-element.429, bf16[384,3072]{1,0:T(8,128)(2,1)} %get-tuple-element.428, bf16[384,3072]{1,0:T(8,128)(2,1)} %get-tuple-element.427, bf16[384,768]{1,0:T(8,128)(2,1)} %get-tuple-element.426, bf16[384,768]{1,0:T(8,128)(2,1)} %get-tuple-element.425, ...), kind=kOutput, calls=%fused_computation.491 | convolution fusion | flops 5464719360 | bytes 13565952 | tf_op jit(solution)/shard_map/rd,rf->df/dot_general | solution.py:160
  572.3 10.5 %fusion.277.refs_0_ = bf16[3072,768]{1,0:T(8,128)(2,1)} fusion(bf16[384,3072]{1,0:T(8,128)(2,1)} %get-tuple-element.420, bf16[384,3072]{1,0:T(8,128)(2,1)} %get-tuple-element.419, bf16[384,3072]{1,0:T(8,128)(2,1)} %get-tuple-element.418, bf16[384,768]{1,0:T(8,128)(2,1)} %get-tuple-element.423, bf16[384,768]{1,0:T(8,128)(2,1)} %get-tuple-element.422, ...), kind=kOutput, calls=%fused_computation.490 | convolution fusion | flops 5464719360 | bytes 13565952 | tf_op jit(solution)/shard_map/rf,rd->fd/dot_general | solution.py:161
  582.8 88.9 %scatter_sums.1 = (f32[192,768]{1,0:T(8,128)}, f32[48,3072]{1,0:T(8,128)}, f32[48,3200]{1,0:T(8,128)}) custom-call(bf16[3072,768]{1,0:T(8,128)(2,1)} %fusion.277.refs_0_, bf16[768,3072]{1,0:T(8,128)(2,1)} %fusion.280.refs_1_, bf16[768,3200]{1,0:T(8,128)(2,1)} %fusion.283.refs_2_), custom_call_target="tpu_custom_call" | custom-call | tf_op jit(solution)/shard_map/scatter_sums/pallas_call | solution.py:580
  (349 shorter events, 169.8 us)
Async XLA Ops:
  94.8 7.8 %copy-start.61 = (s32[2,3]{1,0:T(2,128)S(1)}, s32[2,3]{1,0:T(2,128)}, u32[]{:S(2)}) copy-start(s32[2,3]{1,0:T(2,128)} %param.30) | copy-start | bytes 76
  94.8 10.0 %copy-start.25 = (bf16[1,2,384,768]{3,2,1,0:T(8,128)(2,1)S(1)}, bf16[1,2,384,768]{3,2,1,0:T(8,128)(2,1)}, u32[]{:S(2)}) copy-start(bf16[1,2,384,768]{3,2,1,0:T(8,128)(2,1)} %param.29) | copy-start | bytes 3538948
  108.0 17.7 %copy-start.6 = (f32[384,768]{1,0:T(8,128)}, f32[384,768]{1,0:T(8,128)S(1)}, u32[]{:S(2)}) copy-start(f32[384,768]{1,0:T(8,128)S(1)} %get-tuple-element.800) | copy-start | bytes 3538948 | tf_op jit(solution)/shard_map/cond
  110.2 6.8 copy-start.57
  120.1 10.1 %slice-start.6 = ((s8[4718592]{0:T(1024)(128)(4,1)}), s8[4194304]{0:T(1024)(128)(4,1)S(1)}, s32[]{:S(2)}) async-start(s8[4718592]{0:T(1024)(128)(4,1)} %bitcast.354), calls=%async_computation.6 | async-start | bytes 8388608 | tf_op jit(solution)/shard_map/cond
  121.7 8.6 %slice-start.7 = ((s8[4718592]{0:T(1024)(128)(4,1)}), s8[524288]{0:T(1024)(128)(4,1)S(1)}, s32[]{:S(2)}) async-start(s8[4718592]{0:T(1024)(128)(4,1)} %bitcast.354), calls=%async_computation.7 | async-start | bytes 1048576 | tf_op jit(solution)/shard_map/cond
  128.5 7.3 %slice-start.18 = ((s8[4718592]{0:T(1024)(128)(4,1)}), s8[4194304]{0:T(1024)(128)(4,1)S(1)}, s32[]{:S(2)}) async-start(s8[4718592]{0:T(1024)(128)(4,1)} %bitcast.366), calls=%async_computation.18 | async-start | bytes 8388608 | tf_op jit(solution)/shard_map/cond
  130.3 5.6 slice-start.19
  156.9 2.7 collective-permute-start
  162.6 16.3 %copy-start = (f32[384,768]{1,0:T(8,128)}, f32[384,768]{1,0:T(8,128)S(1)}, u32[]{:S(2)}) copy-start(f32[384,768]{1,0:T(8,128)S(1)} %get-tuple-element.818) | copy-start | bytes 3538948 | tf_op jit(solution)/shard_map/cond
  163.3 6.8 copy-start.59
  170.2 4.7 copy-start.55
  173.3 10.1 %slice-start.8 = ((s8[4718592]{0:T(1024)(128)(4,1)}), s8[4194304]{0:T(1024)(128)(4,1)S(1)}, s32[]{:S(2)}) async-start(s8[4718592]{0:T(1024)(128)(4,1)} %bitcast.356), calls=%async_computation.8 | async-start | bytes 8388608 | tf_op jit(solution)/shard_map/cond
  174.9 8.6 %slice-start.9 = ((s8[4718592]{0:T(1024)(128)(4,1)}), s8[524288]{0:T(1024)(128)(4,1)S(1)}, s32[]{:S(2)}) async-start(s8[4718592]{0:T(1024)(128)(4,1)} %bitcast.356), calls=%async_computation.9 | async-start | bytes 1048576 | tf_op jit(solution)/shard_map/cond
  181.7 7.3 %slice-start.20 = ((s8[4718592]{0:T(1024)(128)(4,1)}), s8[4194304]{0:T(1024)(128)(4,1)S(1)}, s32[]{:S(2)}) async-start(s8[4718592]{0:T(1024)(128)(4,1)} %bitcast.368), calls=%async_computation.20 | async-start | bytes 8388608 | tf_op jit(solution)/shard_map/cond
  183.5 5.6 slice-start.21
  189.0 16.4 %copy-start.56 = (f32[384]{0:T(512)S(1)}, f32[384]{0:T(512)}, u32[]{:S(2)}) copy-start(f32[384]{0:T(512)} %copy-done.55) | copy-start | bytes 4612 | tf_op jit(solution)/shard_map/cond
  189.0 19.0 %copy-start.1 = (f32[384,768]{1,0:T(8,128)S(1)}, f32[384,768]{1,0:T(8,128)}, u32[]{:S(2)}) copy-start(f32[384,768]{1,0:T(8,128)} %copy-done) | copy-start | bytes 3538948 | tf_op jit(solution)/shard_map/cond
  209.3 9.5 %copy-start.2 = (f32[384,768]{1,0:T(8,128)}, f32[384,768]{1,0:T(8,128)S(1)}, u32[]{:S(2)}) copy-start(f32[384,768]{1,0:T(8,128)S(1)} %get-tuple-element.403) | copy-start | bytes 3538948
  211.8 5.6 collective-permute-start.1
  237.0 120.0 %copy-start.10 = (f32[384,768]{1,0:T(8,128)S(1)}, f32[384,768]{1,0:T(8,128)}, u32[]{:S(2)}) copy-start(f32[384,768]{1,0:T(8,128)} %get-tuple-element.772) | copy-start | bytes 3538948
  253.3 99.1 %collective-permute-start.2 = (bf16[18,384]{1,0:T(8,128)(2,1)S(1)}, bf16[18,384]{1,0:T(8,128)(2,1)S(1)}, u32[]{:S(2)}, u32[]{:S(2)}) collective-permute-start(bf16[18,384]{1,0:T(8,128)(2,1)S(1)} %convolution_convert_fusion.7), channel_id=1, source_target_pairs={{16,0},{17,1},{18,2},{19,3},{20,4},{21,5},{22,6},{23,7},{24,8},{25... | collective-permute-start | bytes 41480 | tf_op jit(solution)/shard_map/ppermute | solution.py:24
  357.1 34.0 %copy-start.3 = (f32[384,768]{1,0:T(8,128)S(1)}, f32[384,768]{1,0:T(8,128)}, u32[]{:S(2)}) copy-start(f32[384,768]{1,0:T(8,128)} %copy-done.2) | copy-start | bytes 3538948
  361.4 14.5 %slice-start.26 = ((s8[4718592]{0:T(1024)(128)(4,1)}), s8[4194304]{0:T(1024)(128)(4,1)S(1)}, s32[]{:S(2)}) async-start(s8[4718592]{0:T(1024)(128)(4,1)} %bitcast.374), calls=%async_computation.26 | async-start | bytes 8388608 | tf_op jit(solution)/shard_map/cond
  363.8 12.1 %slice-start.27 = ((s8[4718592]{0:T(1024)(128)(4,1)}), s8[524288]{0:T(1024)(128)(4,1)S(1)}, s32[]{:S(2)}) async-start(s8[4718592]{0:T(1024)(128)(4,1)} %bitcast.374), calls=%async_computation.27 | async-start | bytes 1048576 | tf_op jit(solution)/shard_map/cond
  363.8 18.3 %slice-start.14 = ((s8[4718592]{0:T(1024)(128)(4,1)}), s8[4194304]{0:T(1024)(128)(4,1)S(1)}, s32[]{:S(2)}) async-start(s8[4718592]{0:T(1024)(128)(4,1)} %bitcast.362), calls=%async_computation.14 | async-start | bytes 8388608 | tf_op jit(solution)/shard_map/cond
  375.9 6.1 slice-start.15
  405.0 6.0 slice-start.2
  405.0 6.0 slice-start.3
  405.0 6.0 copy-start.36
  430.6 6.6 copy-start.34
  430.6 6.6 copy-start.44
  430.6 37.1 %copy-start.29 = (f32[18,384]{1,0:T(8,128)S(1)}, f32[18,384]{1,0:T(8,128)}, u32[]{:S(2)}) copy-start(f32[18,384]{1,0:T(8,128)} %copy-done.28) | copy-start | bytes 82948
  430.6 37.1 %copy-start.48 = (f32[384]{0:T(512)S(1)}, f32[384]{0:T(512)}, u32[]{:S(2)}) copy-start(f32[384]{0:T(512)} %copy-done.47) | copy-start | bytes 4612
  430.6 37.1 %copy-start.53 = (f32[384]{0:T(512)S(1)}, f32[384]{0:T(512)}, u32[]{:S(2)}) copy-start(f32[384]{0:T(512)} %copy-done.52) | copy-start | bytes 4612
  430.6 39.5 %copy-start.9 = (f32[384,768]{1,0:T(8,128)S(1)}, f32[384,768]{1,0:T(8,128)}, u32[]{:S(2)}) copy-start(f32[384,768]{1,0:T(8,128)} %copy-done.8) | copy-start | bytes 3538948
  432.2 35.5 %collective-permute-start.3 = (bf16[18,384]{1,0:T(8,128)(2,1)S(1)}, bf16[18,384]{1,0:T(8,128)(2,1)S(1)}, u32[]{:S(2)}, u32[]{:S(2)}) collective-permute-start(bf16[18,384]{1,0:T(8,128)(2,1)S(1)} %convolution_convert_fusion.6), channel_id=1, source_target_pairs={{16,0},{17,1},{18,2},{19,3},{20,4},{21,5},{22,6},{23,7},{24,8},{25... | collective-permute-start | bytes 41480 | tf_op jit(solution)/shard_map/ppermute | solution.py:24
  470.2 36.1 %copy-start.7 = (f32[384,768]{1,0:T(8,128)S(1)}, f32[384,768]{1,0:T(8,128)}, u32[]{:S(2)}) copy-start(f32[384,768]{1,0:T(8,128)} %get-tuple-element.409) | copy-start | bytes 3538948
  474.5 14.5 %slice-start.28 = ((s8[4718592]{0:T(1024)(128)(4,1)}), s8[4194304]{0:T(1024)(128)(4,1)S(1)}, s32[]{:S(2)}) async-start(s8[4718592]{0:T(1024)(128)(4,1)} %bitcast.376), calls=%async_computation.28 | async-start | bytes 8388608 | tf_op jit(solution)/shard_map/cond
  476.9 12.1 %slice-start.29 = ((s8[4718592]{0:T(1024)(128)(4,1)}), s8[524288]{0:T(1024)(128)(4,1)S(1)}, s32[]{:S(2)}) async-start(s8[4718592]{0:T(1024)(128)(4,1)} %bitcast.376), calls=%async_computation.29 | async-start | bytes 1048576 | tf_op jit(solution)/shard_map/cond
  476.9 18.3 %slice-start.16 = ((s8[4718592]{0:T(1024)(128)(4,1)}), s8[4194304]{0:T(1024)(128)(4,1)S(1)}, s32[]{:S(2)}) async-start(s8[4718592]{0:T(1024)(128)(4,1)} %bitcast.364), calls=%async_computation.16 | async-start | bytes 8388608 | tf_op jit(solution)/shard_map/cond
  489.0 6.2 slice-start.17
  515.4 4.3 copy-start.40
  519.7 6.1 slice-start.4
  519.7 6.1 slice-start.5
  543.3 11.9 %copy-start.33 = (bf16[384,768]{1,0:T(8,128)(2,1)}, bf16[384,768]{1,0:T(8,128)(2,1)S(1)}, u32[]{:S(2)}) copy-start(bf16[384,768]{1,0:T(8,128)(2,1)S(1)} %get-tuple-element.438) | copy-start | bytes 1769476
  671.6 6.8 copy-start.21
  671.6 8.3 %copy-start.32 = (f32[48,3072]{1,0:T(8,128)S(1)}, f32[48,3072]{1,0:T(8,128)}, u32[]{:S(2)}) copy-start(f32[48,3072]{1,0:T(8,128)} %get-tuple-element.455) | copy-start | bytes 1769476
  (30 other events, 47.3 us)

commit v2 on v1

v2 whole, which is shorter than its diff:
```python
from functools import partial
import math

import jax
import jax.numpy as jnp
from jax import lax
from jax.experimental import pallas as pl
from jax.experimental.pallas import tpu as pltpu
from jax.sharding import PartitionSpec as P

HEADS = 12
CODE_BITS = 18
GH = 16
GW = 24
LOG2E = math.log2(math.e)


norm_eps = 1e-06


def extent_mask(extent, patches):
    bucket = extent[:, 0:1]
    line_len = jnp.where(bucket == 0, GW, GH)
    position = jnp.arange(patches, dtype=jnp.int32)[None, :]
    inside = (position // line_len < extent[:, 1:2]) & (position % line_len < extent[:, 2:3])
    return inside.astype(jnp.float32)


MESH_ID = pl.DeviceIdType.MESH


def ring_place():
    seg = lax.axis_index("segment")
    here = lax.axis_index("dp")
    core = lax.rem(here, 2)
    col = lax.rem(here // 2, 2)
    row = here // 4
    return seg, here, core, col, row


def meet_neighbours(seg, here, core, col, row, rows):
    barrier = pltpu.get_barrier_semaphore()

    def greet(other):
        pl.semaphore_signal(barrier, inc=1, device_id=(seg, other), device_id_type=MESH_ID)

    greet(here + 1 - 2 * core)
    greet(here + 2 - 4 * col)

    @pl.when(row > 0)
    def _():
        greet(here - 4)

    @pl.when(row < rows - 1)
    def _():
        greet(here + 4)

    has_two = jnp.logical_and(row > 0, row < rows - 1)
    pl.semaphore_wait(barrier, jnp.where(has_two, 4, 3))


def gather_body(rows, *refs):
    n_arr = 3
    shards = refs[:n_arr]
    fulls = refs[n_arr : 2 * n_arr]
    own_sem, send_sem, recv_sem = refs[2 * n_arr :]
    seg, here, core, col, row = ring_place()
    sib = here + 1 - 2 * core
    xn = here + 2 - 4 * col

    def block(arr, src):
        height = shards[arr].shape[0]
        return fulls[arr].at[pl.ds(pl.multiple_of(src * height, height), height)]

    def copy(arr, src, first, slot, to):
        return pltpu.make_async_remote_copy(
            src_ref=shards[arr] if first else block(arr, src),
            dst_ref=block(arr, src),
            send_sem=send_sem.at[arr, slot],
            recv_sem=recv_sem.at[arr, src],
            device_id=(seg, to),
            device_id_type=MESH_ID,
        )

    def arrive(arr, src):
        copy(arr, src, False, 0, sib).wait_recv()

    def index(src_row, src_col):
        return (src_row * 2 + src_col) * 2 + core

    def to_sib(arr, src_row, src_col, first=False):
        return copy(arr, index(src_row, src_col), first, 3 * rows + src_row * 2 + src_col, sib)

    def to_x(arr, src_row, first=False):
        return copy(arr, index(src_row, col), first, 2 * rows + src_row, xn)

    def to_up(arr, src_row, first=False):
        return copy(arr, index(src_row, col), first, src_row, here + 4)

    def to_down(arr, src_row, first=False):
        return copy(arr, index(src_row, col), first, rows + src_row, here - 4)

    def own_copy(arr):
        return pltpu.make_async_copy(shards[arr], block(arr, here), own_sem.at[arr])

    def own(arr):
        @pl.when(row < rows - 1)
        def _():
            to_up(arr, row, True).start()

        @pl.when(row > 0)
        def _():
            to_down(arr, row, True).start()

        to_x(arr, row, True).start()
        to_sib(arr, row, col, True).start()
        own_copy(arr).start()

    def away(arr, dist):
        @pl.when(row - dist >= 0)
        def _():
            src_row = row - dist
            arrive(arr, index(src_row, col))

            @pl.when(row < rows - 1)
            def _():
                to_up(arr, src_row).start()

            to_x(arr, src_row).start()
            to_sib(arr, src_row, col).start()

        @pl.when(row + dist < rows)
        def _():
            src_row = row + dist
            arrive(arr, index(src_row, col))

            @pl.when(row > 0)
            def _():
                to_down(arr, src_row).start()

            to_x(arr, src_row).start()
            to_sib(arr, src_row, col).start()

    def across(arr):
        def at(src_row):
            arrive(arr, index(src_row, 1 - col))
            to_sib(arr, src_row, 1 - col).start()

        at(row)
        for dist in range(1, rows):
            pl.when(row - dist >= 0)(lambda: at(row - dist))
            pl.when(row + dist < rows)(lambda: at(row + dist))

    meet_neighbours(seg, here, core, col, row, rows)
    for arr in range(n_arr):
        own(arr)
        if arr > 0:
            away(arr - 1, rows - 1)
        away(arr, 1)
        if arr > 0:
            across(arr - 1)
        for dist in range(2, rows - 1):
            away(arr, dist)
    away(n_arr - 1, rows - 1)
    across(n_arr - 1)
    for arr in range(n_arr):
        own_copy(arr).wait()

        @pl.loop(0, 2 * rows)
        def _(i):
            copy(arr, 2 * i + 1 - core, False, 0, sib).wait_recv()
            copy(arr, 2 * i + core, False, 3 * rows + i, sib).wait_send()

        @pl.loop(0, rows)
        def _(i):
            to_x(arr, i).wait_send()

            @pl.when(jnp.logical_and(i <= row, row < rows - 1))
            def _():
                to_up(arr, i).wait_send()

            @pl.when(jnp.logical_and(i >= row, row > 0))
            def _():
                to_down(arr, i).wait_send()


def gather_blocks(shards):
    count = lax.axis_size("dp")
    rows = count // 4
    any_spec = pl.BlockSpec(memory_space=pl.ANY)
    return pl.pallas_call(
        partial(gather_body, rows),
        out_shape=tuple(
            jax.ShapeDtypeStruct((count * s.shape[0], s.shape[1]), s.dtype) for s in shards
        ),
        in_specs=[any_spec] * 3,
        out_specs=(any_spec,) * 3,
        scratch_shapes=[
            pltpu.SemaphoreType.DMA((3,)),
            pltpu.SemaphoreType.DMA((3, 5 * rows)),
            pltpu.SemaphoreType.DMA((3, 4 * rows)),
        ],
        compiler_params=pltpu.CompilerParams(collective_id=1, has_side_effects=True),
        name="gather_weights",
    )(*shards)


def scatter_body(rows, *refs):
    n_arr = 3
    parts = refs[:n_arr]
    outs = refs[n_arr : 2 * n_arr]
    own, sibs, xsend, xrecv, zsend, zrecv = [
        refs[(2 + i) * n_arr : (3 + i) * n_arr] for i in range(6)
    ]
    own_sem, sib_ssem, sib_rsem, x_ssem, x_rsem, z_ssem, z_rsem = refs[8 * n_arr :]
    seg, here, core, col, row = ring_place()
    sib = here + 1 - 2 * core
    xn = here + 2 - 4 * col

    def block(arr, dst):
        height = outs[arr].shape[0]
        return parts[arr].at[pl.ds(pl.multiple_of(dst * height, height), height)]

    def remote(src, dst, ssem, rsem, to):
        return pltpu.make_async_remote_copy(
            src_ref=src,
            dst_ref=dst,
            send_sem=ssem,
            recv_sem=rsem,
            device_id=(seg, to),
            device_id_type=MESH_ID,
        )

    def own_copy(arr, place):
        return pltpu.make_async_copy(
            block(arr, 2 * place + core), own[arr].at[place], own_sem.at[arr, place]
        )

    def sib_copy(arr, place):
        return remote(
            block(arr, 2 * place + 1 - core),
            sibs[arr].at[place],
            sib_ssem.at[arr, place],
            sib_rsem.at[arr, place],
            sib,
        )

    def x_copy(arr, dst_row):
        return remote(
            xsend[arr].at[dst_row],
            xrecv[arr].at[dst_row],
            x_ssem.at[arr, dst_row],
            x_rsem.at[arr, dst_row],
            xn,
        )

    def z_copy(arr, way, dst_row):
        return remote(
            zsend[arr].at[dst_row],
            zrecv[arr].at[way, dst_row],
            z_ssem.at[arr, dst_row],
            z_rsem.at[arr, way, dst_row],
            here + 4 - 8 * way,
        )

    def each_far(body):
        @pl.loop(0, 2 * (rows - 1))
        def _(i):
            way = lax.rem(i, 2)
            dst_row = row + (1 - 2 * way) * (rows - 1 - i // 2)
            pl.when(jnp.logical_and(dst_row >= 0, dst_row < rows))(lambda: body(way, dst_row))

    def start_pairs(arr):
        def go(dst_row, at_col):
            sib_copy(arr, 2 * dst_row + at_col).start()
            own_copy(arr, 2 * dst_row + at_col).start()

        each_far(lambda way, dst_row: go(dst_row, 1 - col))
        go(row, 1 - col)
        each_far(lambda way, dst_row: go(dst_row, col))
        go(row, col)

    def pair_sum(arr, place):
        sib_copy(arr, place).wait_recv()
        own_copy(arr, place).wait()
        return own[arr][place].astype(jnp.float32) + sibs[arr][place].astype(jnp.float32)

    def x_stage(arr):
        def go(dst_row):
            xsend[arr][dst_row] = pair_sum(arr, 2 * dst_row + 1 - col).astype(jnp.bfloat16)
            x_copy(arr, dst_row).start()

        each_far(lambda way, dst_row: go(dst_row))
        go(row)

    def column_sum(arr, dst_row):
        x_copy(arr, dst_row).wait_recv()
        return pair_sum(arr, 2 * dst_row + col) + xrecv[arr][dst_row].astype(jnp.float32)

    def z_stage(arr):
        def go(way, dst_row):
            behind = row - 1 + 2 * way

            @pl.when(jnp.logical_and(behind >= 0, behind < rows))
            def _():
                z_copy(arr, way, dst_row).wait_recv()

            total = column_sum(arr, dst_row) + zrecv[arr][way, dst_row].astype(jnp.float32)
            zsend[arr][dst_row] = total.astype(jnp.bfloat16)
            z_copy(arr, way, dst_row).start()

        each_far(go)

        @pl.when(row > 0)
        def _():
            z_copy(arr, 0, row).wait_recv()

        @pl.when(row < rows - 1)
        def _():
            z_copy(arr, 1, row).wait_recv()

        outs[arr][...] = (
            column_sum(arr, row)
            + zrecv[arr][0, row].astype(jnp.float32)
            + zrecv[arr][1, row].astype(jnp.float32)
        )

    meet_neighbours(seg, here, core, col, row, rows)
    for arr in range(n_arr):
        start_pairs(arr)

    def clear(way):
        for arr in range(n_arr):
            zrecv[arr][way] = jnp.zeros(zrecv[arr].shape[1:], jnp.bfloat16)

    pl.when(row == 0)(lambda: clear(0))
    pl.when(row == rows - 1)(lambda: clear(1))
    x_stage(0)
    for arr in range(n_arr):
        if arr + 1 < n_arr:
            x_stage(arr + 1)
        z_stage(arr)
    for arr in range(n_arr):

        @pl.loop(0, 2 * rows)
        def _(i):
            sib_copy(arr, i).wait_send()

        @pl.loop(0, rows)
        def _(i):
            x_copy(arr, i).wait_send()

        each_far(lambda way, dst_row: z_copy(arr, way, dst_row).wait_send())


def scatter_sums(parts):
    count = lax.axis_size("dp")
    rows = count // 4
    any_spec = pl.BlockSpec(memory_space=pl.ANY)
    vmem_spec = pl.BlockSpec(memory_space=pltpu.VMEM)
    shapes = [(p.shape[0] // count, p.shape[1]) for p in parts]

    def buffers(*lead):
        return [pltpu.VMEM(lead + s, jnp.bfloat16) for s in shapes]

    dma = pltpu.SemaphoreType.DMA
    return pl.pallas_call(
        partial(scatter_body, rows),
        out_shape=tuple(jax.ShapeDtypeStruct(s, jnp.float32) for s in shapes),
        in_specs=[any_spec] * 3,
        out_specs=(vmem_spec,) * 3,
        scratch_shapes=buffers(2 * rows)
        + buffers(2 * rows)
        + buffers(rows)
        + buffers(rows)
        + buffers(rows)
        + buffers(2, rows)
        + [
            dma((3, 2 * rows)),
            dma((3, 2 * rows)),
            dma((3, 2 * rows)),
            dma((3, rows)),
            dma((3, rows)),
            dma((3, rows)),
            dma((3, 2, rows)),
        ],
        compiler_params=pltpu.CompilerParams(
            collective_id=2, has_side_effects=True, vmem_limit_bytes=56 << 20
        ),
        name="scatter_sums",
    )(*parts)


def dot_nn(left, right):
    return lax.dot_general(left, right, (((1,), (0,)), ((), ())), preferred_element_type=jnp.float32)


def dot_nt(left, right):
    return lax.dot_general(left, right, (((1,), (1,)), ((), ())), preferred_element_type=jnp.float32)


def dot_tn(left, right):
    return lax.dot_general(left, right, (((0,), (0,)), ((), ())), preferred_element_type=jnp.float32)


def low(array):
    return array.astype(jnp.bfloat16)


def wide(array):
    return array.astype(jnp.float32)


def row_sum(array):
    return jnp.sum(array, 0, keepdims=True)


def row_mean(array):
    return jnp.mean(array, -1, keepdims=True)


def blocks_body(*refs):
    (
        attn_hbm, up_hbm, down_hbm, x_ref, mask_ref,
        seg_out, g_down, g_up, g_attn, stats,
        w_attn, w_up, w_down, norms, maps,
        h_buf, out_buf, xhat1, rstd1, xhat2, rstd2, a_s, qkv_s, mixed_s, c_s, act_s, slope_s,
        lse_pack, bias_pack, gm_s, go_s, gmix_s, enc_s, u_s, small_acc, stage, relay_tx, relay_rx,
        w_sem, out_sem, stage_sem, relay_ssem, relay_rsem,
    ) = refs
    seg = lax.axis_index("segment")
    here = lax.axis_index("dp")
    is_enc = seg == 0
    is_dec = seg == 1
    total_rows, features = x_ref.shape
    images = out_buf.shape[0]
    patches = total_rows // images
    hidden = w_up.shape[1]
    head_dim = features // HEADS
    pairs = features // 128
    chunk = features
    code_rows = relay_tx.shape[1]

    def rows(m):
        return pl.ds(pl.multiple_of(m * patches, patches), patches)

    def cols(j, width):
        return pl.ds(pl.multiple_of(j * width, width), width)

    def weight_copies():
        return [
            pltpu.make_async_copy(src, dst, w_sem.at[i])
            for i, (src, dst) in enumerate(
                ((attn_hbm, w_attn), (up_hbm, w_up), (down_hbm, w_down))
            )
        ]

    def relay(m):
        return pltpu.make_async_remote_copy(
            src_ref=relay_tx.at[m],
            dst_ref=relay_rx.at[m],
            send_sem=relay_ssem.at[m],
            recv_sem=relay_rsem.at[m],
            device_id=(1 - seg, here),
            device_id_type=MESH_ID,
        )

    def result(m):
        return pltpu.make_async_copy(out_buf.at[m], seg_out.at[rows(m)], out_sem.at[m])

    def energy(slot, tensor, keep):
        square = row_sum(tensor * tensor * keep)
        total = square[:, :128]
        for j in range(1, pairs):
            total = total + square[:, j * 128 : (j + 1) * 128]
        stats[slot : slot + 1, :] += total

    def code_mask(array):
        return jnp.where(
            lax.broadcasted_iota(jnp.int32, array.shape, 0) < CODE_BITS, array, 0.0
        )

    def normalize(values, xhat, rstd, rs, slot):
        gain, bias = norms[slot : slot + 1, :], norms[slot + 1 : slot + 2, :]
        centered = values - row_mean(values)
        scale = lax.rsqrt(row_mean(centered * centered) + norm_eps)
        hat = centered * scale
        xhat[rs, :] = low(hat)
        rstd[rs, :] = scale
        return low(hat * gain + bias)

    def norm_back(grad, xhat, rstd, rs, norm):
        gain, slot = norms[norm : norm + 1, :], code_rows + norm
        hat = wide(xhat[rs, :])
        small_acc[slot : slot + 1, :] += row_sum(grad * hat)
        small_acc[slot + 1 : slot + 2, :] += row_sum(grad)
        scaled = grad * gain
        return rstd[rs, :] * (scaled - row_mean(scaled) - hat * row_mean(scaled * hat))

    lane = lax.broadcasted_iota(jnp.int32, (1, 128), 1)
    halves = [low(wide(lane < head_dim)), low(wide(lane >= head_dim))]
    in_first = lax.broadcasted_iota(jnp.int32, (patches, 128), 1) < head_dim

    def head_row(head):
        return low(wide(jnp.logical_and(lane < 48, lax.rem(lane, 16) == head)))

    def three_terms(values):
        first = wide(low(values))
        rest = values - first
        second = wide(low(rest))
        third = wide(low(rest - second))
        return jnp.where(lane < 16, first, jnp.where(lane < 32, second, third))

    def forward(m, _):
        rs = rows(m)

        @pl.when(is_enc)
        def _():
            h_buf[...] = wide(x_ref[rs, :])

        @pl.when(is_dec)
        def _():
            relay(m).wait_recv()
            h_buf[...] = dot_tn(relay_rx[m], maps[...])

        keep = jnp.concatenate([mask_ref[rs, :]] * pairs, axis=1)
        bias_pack[rs, :] = low(jnp.where(lane == 48, (1.0 - mask_ref[rs, :]) * -1e30, 0.0))
        a_s[rs, :] = normalize(h_buf[...], xhat1, rstd1, rs, 0)
        for j in range(3):
            part = dot_nn(a_s[rs, :], w_attn[:, j * features : (j + 1) * features])
            if j == 0:
                part = part * (LOG2E / math.sqrt(head_dim))
            qkv_s[rs, j * features : (j + 1) * features] = low(part)
        one_lane = low(wide(jnp.broadcast_to(lane == 48, (patches, 128))))

        def heads(j, lse):
            query = qkv_s[rs, cols(j, 128)]
            key = qkv_s[rs, cols(j + pairs, 128)]
            value = qkv_s[rs, cols(j + 2 * pairs, 128)]
            query = jnp.concatenate([query, one_lane], axis=1)
            outs = []
            for i in range(2):
                keys_one = jnp.concatenate([key * halves[i], bias_pack[rs, :]], axis=1)
                scores = dot_nt(query, keys_one)
                top = jnp.max(scores, -1, keepdims=True)
                weight = low(jnp.exp2(scores - top))
                mixed = dot_nn(weight, value * halves[i] + halves[1 - i])
                count = mixed[:, (1 - i) * head_dim : (1 - i) * head_dim + 1]
                outs.append(mixed * (1.0 / count))
                head = 2 * j + i
                lse = jnp.where(
                    jnp.logical_and(lane < 48, lax.rem(lane, 16) == head),
                    top + jnp.log2(count),
                    lse,
                )
            mixed_s[rs, cols(j, 128)] = low(jnp.where(in_first, outs[0], outs[1]))
            return lse

        lse = lax.fori_loop(0, pairs, heads, jnp.zeros((patches, 128), jnp.float32))
        lse_pack[rs, :] = low(
            jnp.where(lane < 48, three_terms(-lse), jnp.where(lane == 48, 1.0, 0.0))
        )
        attn_out = dot_nn(mixed_s[rs, :], w_attn[:, 3 * features : 4 * features])
        energy(1, attn_out, keep)
        h_buf[...] += attn_out
        c_s[rs, :] = normalize(h_buf[...], xhat2, rstd2, rs, 2)

        def up(j, _):
            pre = dot_nn(c_s[rs, :], w_up[:, cols(j, chunk)])
            phi = 0.5 + 0.5 * lax.erf(pre * math.sqrt(0.5))
            act_s[rs, cols(j, chunk)] = low(pre * phi)
            slope_s[rs, cols(j, chunk)] = low(
                phi + pre * (jnp.exp(-0.5 * pre * pre) * (1.0 / math.sqrt(2.0 * math.pi)))
            )
            return 0

        lax.fori_loop(0, hidden // chunk, up, 0)
        mlp_out = dot_nn(act_s[rs, :], w_down[...])
        energy(2, mlp_out, keep)
        block_out = h_buf[...] + mlp_out
        energy(0, block_out, keep)
        stats[3:4, :] += row_sum(mask_ref[rs, :])

        @pl.when(is_enc)
        def _():
            enc_s[rs, :] = low(block_out)
            code_pre = code_mask(dot_nt(maps[...], enc_s[rs, :]))
            u_s[m] = code_pre
            scale = lax.rsqrt(row_sum(code_pre * code_pre) + 1.0)
            relay_tx[m] = low(jnp.tanh(2.0 * math.sqrt(CODE_BITS) * (code_pre * scale)))
            relay(m).start()

        @pl.when(is_dec)
        def _():
            out_buf[m] = block_out
            result(m).start()

        return 0

    def backward(step, _):
        m = images - 1 - step
        rs = rows(m)

        @pl.when(is_enc)
        def _():
            relay(m).wait_recv()
            code_pre = u_s[m]
            scale = lax.rsqrt(row_sum(code_pre * code_pre) + 1.0)
            unit = code_pre * scale
            factor = 2.0 * math.sqrt(CODE_BITS)
            bent = jnp.tanh(factor * unit)
            g_unit = wide(relay_rx[m]) * (factor * (1.0 - bent * bent))
            g_u = low((g_unit - unit * row_sum(g_unit * unit)) * scale)
            small_acc[0:code_rows, :] += dot_nn(g_u, enc_s[rs, :])
            h_buf[...] = dot_tn(g_u, maps[...])

        @pl.when(is_dec)
        def _():
            h_buf[...] = wide(x_ref[rs, :])

        gm_s[rs, :] = low(h_buf[...])

        def down(j, _):
            g_act = dot_nt(gm_s[rs, :], w_down[cols(j, chunk), :])
            slope_s[rs, cols(j, chunk)] = low(g_act * wide(slope_s[rs, cols(j, chunk)]))
            return 0

        lax.fori_loop(0, hidden // chunk, down, 0)
        g_c = dot_nt(slope_s[rs, :], w_up[...])
        h_buf[...] += norm_back(g_c, xhat2, rstd2, rs, 2)
        go_s[rs, :] = low(h_buf[...])
        gmix_s[...] = low(dot_nt(go_s[rs, :], w_attn[:, 3 * features : 4 * features]))
        product = wide(gmix_s[...]) * wide(mixed_s[rs, :])
        high = low(product)
        head_of = lax.broadcasted_iota(jnp.int32, (features, 128), 0) // head_dim
        lane_of = lax.broadcasted_iota(jnp.int32, (features, 128), 1)
        pick = low(wide(jnp.logical_and(lane_of < 48, lax.rem(lane_of, 16) == head_of)))
        inner = dot_nn(high, pick) + dot_nn(low(product - wide(high)), pick)
        inner_pack = low(three_terms(-inner))

        def heads(j, _):
            at = [cols(j + i * pairs, 128) for i in range(3)]
            query, key, value = [qkv_s[rs, place] for place in at]
            g_mixed = gmix_s[:, cols(j, 128)]
            query_more = jnp.concatenate([query, lse_pack[rs, :]], axis=1)
            g_more = jnp.concatenate([g_mixed, inner_pack], axis=1)
            found = []
            for i in range(2):
                extra = bias_pack[rs, :] + head_row(2 * j + i)
                probs = jnp.exp2(
                    dot_nt(query_more, jnp.concatenate([key * halves[i], extra], axis=1))
                )
                g_probs = dot_nt(g_more, jnp.concatenate([value * halves[i], extra], axis=1))
                probs_low = low(probs)
                g_scores = low(probs * g_probs)
                found.append(
                    (
                        dot_nn(g_scores, key),
                        dot_tn(g_scores, query),
                        dot_tn(probs_low, g_mixed),
                    )
                )
            scales = (1.0 / math.sqrt(head_dim), 1.0 / LOG2E, 1.0)
            for i in range(3):
                joined = jnp.where(in_first, found[0][i], found[1][i])
                qkv_s[rs, at[i]] = low(joined * scales[i])
            return 0

        lax.fori_loop(0, pairs, heads, 0)
        g_a = dot_nt(qkv_s[rs, :], w_attn[:, : 3 * features])
        g_h = h_buf[...] + norm_back(g_a, xhat1, rstd1, rs, 0)

        @pl.when(is_enc)
        def _():
            out_buf[m] = g_h
            result(m).start()

        @pl.when(is_dec)
        def _():
            g_z = low(g_h)
            small_acc[0:code_rows, :] += dot_nn(relay_rx[m], g_z)
            relay_tx[m] = low(code_mask(dot_nt(maps[...], g_z)))
            relay(m).start()

        return 0

    barrier = pltpu.get_barrier_semaphore()
    pl.semaphore_signal(barrier, inc=1, device_id=(1 - seg, here), device_id_type=MESH_ID)
    for copy in weight_copies():
        copy.start()
    stats[...] = jnp.zeros_like(stats)
    small_acc[...] = jnp.zeros_like(small_acc)
    pl.semaphore_wait(barrier, 1)
    for copy in weight_copies():
        copy.wait()
    small = wide(w_attn[:, 4 * features :]).T
    maps[...] = low(code_mask(small[:code_rows]))
    norms[0:4, :] = small[CODE_BITS : CODE_BITS + 4]
    lax.fori_loop(0, images, forward, 0)
    lax.fori_loop(0, images, backward, 0)

    tasks = []
    for j in range(hidden // chunk):
        at = slice(j * chunk, (j + 1) * chunk)
        tasks.append((act_s, at, gm_s, slice(None), g_down.at[at]))
    for j in range(hidden // chunk):
        at = slice(j * chunk, (j + 1) * chunk)
        tasks.append((c_s, slice(None), slope_s, at, g_up.at[:, at]))
    for j in range(3):
        at = slice(j * features, (j + 1) * features)
        tasks.append((a_s, slice(None), qkv_s, at, g_attn.at[:, at]))
    tasks.append(
        (mixed_s, slice(None), go_s, slice(None), g_attn.at[:, 3 * features : 4 * features])
    )
    pending = []
    for i, (left, left_at, right, right_at, place) in enumerate(tasks):
        if i >= 2:
            pending[i - 2].wait()
        stage[i % 2] = low(dot_tn(left[:, left_at], right[:, right_at]))
        pending.append(pltpu.make_async_copy(stage.at[i % 2], place, stage_sem.at[i % 2]))
        pending[i].start()
    pending[-2].wait()
    small_grad = jnp.concatenate(
        [
            small_acc[0:CODE_BITS, :],
            small_acc[code_rows : code_rows + 4, :],
            jnp.zeros((128 - CODE_BITS - 4, features), jnp.float32),
        ],
        axis=0,
    ).T
    stage[len(tasks) % 2, :, :128] = low(small_grad)
    last = pltpu.make_async_copy(
        stage.at[len(tasks) % 2, :, pl.ds(0, 128)],
        g_attn.at[:, pl.ds(4 * features, 128)],
        stage_sem.at[len(tasks) % 2],
    )
    last.start()
    pending[-1].wait()
    last.wait()
    for m in range(images):
        result(m).wait()
        relay(m).wait_send()


def run_blocks(attn_all, up_all, down_all, x, mask):
    images, patches, features = x.shape
    total = images * patches
    hidden = up_all.shape[1]
    code_rows = -(-CODE_BITS // 16) * 16
    bf16, f32 = jnp.bfloat16, jnp.float32
    any_spec = pl.BlockSpec(memory_space=pl.ANY)
    vmem_spec = pl.BlockSpec(memory_space=pltpu.VMEM)
    dma = pltpu.SemaphoreType.DMA
    scratch = [
        (attn_all.shape, bf16), (up_all.shape, bf16), (down_all.shape, bf16),
        ((8, features), f32), ((code_rows, features), bf16),
        ((patches, features), f32), ((images, patches, features), f32),
        ((total, features), bf16), ((total, 1), f32), ((total, features), bf16), ((total, 1), f32),
        ((total, features), bf16), ((total, 3 * features), bf16), ((total, features), bf16),
        ((total, features), bf16), ((total, hidden), bf16), ((total, hidden), bf16),
        ((total, 128), bf16), ((total, 128), bf16),
        ((total, features), bf16), ((total, features), bf16), ((patches, features), bf16),
        ((total, features), bf16), ((images, code_rows, patches), f32),
        ((code_rows + 8, features), f32), ((2, features, features), bf16),
        ((images, code_rows, patches), bf16), ((images, code_rows, patches), bf16),
    ]
    return pl.pallas_call(
        blocks_body,
        out_shape=(
            jax.ShapeDtypeStruct((total, features), f32),
            jax.ShapeDtypeStruct(down_all.shape, bf16),
            jax.ShapeDtypeStruct(up_all.shape, bf16),
            jax.ShapeDtypeStruct(attn_all.shape, bf16),
            jax.ShapeDtypeStruct((8, 128), f32),
        ),
        in_specs=[any_spec] * 3 + [vmem_spec] * 2,
        out_specs=(any_spec,) * 4 + (vmem_spec,),
        scratch_shapes=[pltpu.VMEM(s, t) for s, t in scratch]
        + [dma((3,)), dma((images,)), dma((2,)), dma((images,)), dma((images,))],
        compiler_params=pltpu.CompilerParams(
            collective_id=3, has_side_effects=True, vmem_limit_bytes=60 << 20
        ),
        name="both_blocks",
    )(attn_all, up_all, down_all, x.reshape(total, features), mask)


def on_device(
    segment_input,
    image_extent,
    norm1_gain,
    norm1_bias,
    norm2_gain,
    norm2_bias,
    qkv_weight,
    out_weight,
    up_weight,
    down_weight,
    code_maps,
):
    _, images, patches, features = segment_input.shape
    qkv_width = qkv_weight.shape[2]
    small = jnp.concatenate(
        [code_maps[0]]
        + [v[0][:, None] for v in (norm1_gain, norm1_bias, norm2_gain, norm2_bias)],
        axis=1,
    )
    small = jnp.pad(small, ((0, 0), (0, 128 - small.shape[1])))
    shards = (
        jnp.concatenate([qkv_weight[0], out_weight[0], small], axis=1),
        up_weight[0],
        down_weight[0],
    )
    by_kernel = shards[0].shape[0] % 16 == 0
    if by_kernel:
        attn_all, up_all, down_all = gather_blocks(shards)
    else:
        attn_all, up_all, down_all = [lax.all_gather(s, "dp", axis=0, tiled=True) for s in shards]
    validity = extent_mask(image_extent, patches)
    mask = jnp.broadcast_to(validity.reshape(-1, 1), (images * patches, 128))
    segment_output, down_grad, up_grad, attn_grad, stats = run_blocks(
        attn_all, up_all, down_all, segment_input[0], mask
    )
    parts = (down_grad, up_grad, attn_grad)
    if by_kernel:
        down_shard, up_shard, attn_shard = scatter_sums(parts)
    else:
        down_shard, up_shard, attn_shard = [
            lax.psum_scatter(v.astype(jnp.float32), "dp", scatter_dimension=0, tiled=True)
            for v in parts
        ]
    stats = lax.psum(stats, "dp")
    small_shard = attn_shard[:, qkv_width + features :]
    norm_shards = [small_shard[:, CODE_BITS + i][None] for i in range(4)]
    rms_stats = jnp.sqrt(jnp.sum(stats[:3], 1) / (stats[3, 0] * features))[None]
    return (
        segment_output.reshape(segment_input.shape),
        rms_stats,
        norm_shards[0],
        norm_shards[1],
        norm_shards[2],
        norm_shards[3],
        attn_shard[:, :qkv_width][None],
        attn_shard[:, qkv_width : qkv_width + features][None],
        up_shard[None],
        down_shard[None],
        small_shard[:, :CODE_BITS][None],
    )


def solution(mesh):
    return jax.shard_map(
        on_device,
        mesh=mesh,
        in_specs=(
            P("segment", "dp", None, None),
            P("dp", None),
            P("segment", "dp"),
            P("segment", "dp"),
            P("segment", "dp"),
            P("segment", "dp"),
            P("segment", "dp", None),
            P("segment", "dp", None),
            P("segment", "dp", None),
            P("segment", "dp", None),
            P("segment", "dp", None),
        ),
        out_specs=(
            P("segment", "dp", None, None),
            P("segment", None),
            P("segment", "dp"),
            P("segment", "dp"),
            P("segment", "dp"),
            P("segment", "dp"),
            P("segment", "dp", None),
            P("segment", "dp", None),
            P("segment", "dp", None),
            P("segment", "dp", None),
            P("segment", "dp", None),
        ),
        check_vma=False,
    )
```

time: 688 us -> 357 us (0.52)
  matrix products: 192 us -> 0 us
  Pallas kernels: 176 us -> 306 us
  other arithmetic: 98.7 us -> 3.61 us
  waiting for transfers between devices: 94 us -> 0 us
  local copies, waits for them, and re-layouts: 69.6 us -> 16.6 us
  loops' own time: 10.8 us -> 0 us
  starting transfers between devices: 8.06 us -> 0 us
    dot_general x51 -> x0, matrix products: 192 us -> none  [the longest x2 29.8 us: mlp_forward(): jnp.dot(activation, w_down, preferred_element_type=jnp.float32)]
    pallas_call x0 -> x1, Pallas kernels: none -> 129 us  [run_blocks(): pl.pallas_call(blocks_body, out_shape=(jax.ShapeDtypeStruct((total, featu...]
    ppermute x4 -> x0, waiting for transfers between devices: 94 us -> none  [passed_along(): return lax.ppermute(array, axis, pairs)]
    convert_element_type x30 -> x1, other arithmetic: 43.6 us -> 0.13 us  [extent_mask(): return inside.astype(jnp.float32)]
    another operation x27 -> x0, local copies, waits for them, and re-layouts: 31.9 us -> none
    reduce_sum x27 -> x1, other arithmetic: 29.5 us -> 0.11 us  [on_device(): rms_stats = jnp.sqrt(jnp.sum(stats[:3], 1) / (stats[3, 0] * features))[None]]
    another operation x9 -> x0, loops' own time: 10.8 us -> none  [the longest x3 9.52 us: on_device(): lax.cond(active, attention_backward, blank_attention, grad_mid, saved_ten...]
    another operation x8 -> x0, other arithmetic: 8.46 us -> none  [the longest x2 4.03 us: block_forward(): jnp.stack([energy(block_result, row_mask), energy(attn_out, row_mask), en...]
  transfers between devices with their start and end apart: 4 -> 0, of which waited for: 4 -> 0; matrix products, arithmetic and copies ran while one was open for 1% -> 0% of each run, Pallas kernels for 0% -> 0%
where the time goes in v2:
time: 357 us
  Pallas kernels  306 us (86%)
  blocking collectives  29.5 us (8%)
  local copies, waits for them, and re-layouts  16.6 us (5%)
  other arithmetic  3.61 us (1%)
    pallas_call x1, Pallas kernels, run_blocks(): pl.pallas_call(blocks_body, out_shape=(jax.ShapeDtypeStruct((total, featu...  129 us
    pallas_call x1, Pallas kernels, scatter_sums(): pl.pallas_call(partial(scatter_body, rows), out_shape=tuple((jax.ShapeDty...  88.9 us
    pallas_call x1, Pallas kernels, gather_blocks(): pl.pallas_call(partial(gather_body, rows), out_shape=tuple((jax.ShapeDtyp...  87.5 us
    psum x1, blocking collectives, on_device(): stats = lax.psum(stats, 'dp')  29.5 us

profile of v2, /device:TPU:0, one launch (start us, length us, event | category | flops | bytes accessed | tf_op | source)
XLA Modules:
  0.0 356.9 jit_solution(3201497115478603955)
XLA Ops:
  0.7 1.0 sign_reduce_fusion
  1.7 0.1 broadcast_compare_fusion
  1.8 0.1 rem.67
  1.9 0.1 rem.71
  2.0 0.1 lt.45
  2.0 0.1 lt.40
  2.1 0.1 fusion.6
  2.3 0.8 copy.29
  3.0 0.8 copy.30
  3.8 0.8 copy.31
  4.5 0.8 copy.32
  5.3 0.8 copy.28
  6.1 0.1 concatenate.6
  6.2 1.7 fusion.1.refs_0_
  7.9 0.9 broadcast_in_dim.32.refs_4_
  8.8 87.5 %gather_weights.1 = (bf16[768,3200]{1,0:T(8,128)(2,1)}, bf16[768,3072]{1,0:T(8,128)(2,1)}, bf16[3072,768]{1,0:T(8,128)(2,1)}) custom-call(bf16[48,3200]{1,0:T(8,128)(2,1)} %fusion.1.refs_0_, bf16[48,3072]{1,0:T(8,128)(2,1)} %bitcast.30, bf16[192,768]{1,0:T(8,128)(2,1)} %bitcast.31), custom_call_target="tpu_custom_call" | custom-call | tf_op jit(solution)/shard_map/gather_weights/pallas_call | solution.py:191
  96.3 129.5 %both_blocks.1 = (f32[768,768]{1,0:T(8,128)}, bf16[3072,768]{1,0:T(8,128)(2,1)}, bf16[768,3072]{1,0:T(8,128)(2,1)}, bf16[768,3200]{1,0:T(8,128)(2,1)}, f32[8,128]{1,0:T(8,128)}) custom-call(bf16[768,3200]{1,0:T(8,128)(2,1)} %get-tuple-element.22.refs_0_, bf16[768,3072]{1,0:T(8,128)(2,1)} %get-tuple-element.23.refs_1_, ...), custom_call_target="tpu_custom_call" | custom-call | tf_op jit(solution)/shard_map/both_blocks/pallas_call | solution.py:767
  225.8 29.5 %psum.7 = f32[8,128]{1,0:T(8,128)S(1)} all-reduce(f32[8,128]{1,0:T(8,128)} %get-tuple-element.26), channel_id=1, replica_groups=mesh['segment'=2,'dp'=16] {'dp'}, use_global_device_ids=true, to_apply=%region_0.1 | all-reduce | flops 1024 | bytes 8192 | tf_op jit(solution)/shard_map/psum | solution.py:831
  255.3 0.5 slice.46
  256.4 0.1 slice_reduce_fusion.4
  256.6 0.5 sqrt_bitcast_fusion
  257.1 0.0 copy-start
  257.1 88.9 %scatter_sums.1 = (f32[192,768]{1,0:T(8,128)}, f32[48,3072]{1,0:T(8,128)}, f32[48,3200]{1,0:T(8,128)}) custom-call(bf16[3072,768]{1,0:T(8,128)(2,1)} %get-tuple-element.27.refs_0_, bf16[768,3072]{1,0:T(8,128)(2,1)} %get-tuple-element.28.refs_1_, bf16[768,3200]{1,0:T(8,128)(2,1)} %get-tuple-element.29.refs_2_), custom_call_target="tpu_custom_call" | custom-call | tf_op jit(solution)/shard_map/scatter_sums/pallas_call | solution.py:367
  346.0 0.0 copy-start.2
  346.0 0.0 copy-start.1
  346.0 1.7 slice_reduce_fusion
  347.7 1.3 slice_bitcast_fusion.2
  349.1 1.4 copy.33
  350.5 1.6 slice_bitcast_fusion.1
  352.1 1.8 slice_bitcast_fusion
  353.9 0.0 copy-done
  353.9 1.4 copy.37
  355.3 0.0 copy-done.2
  355.3 0.8 copy.38
  356.1 0.0 copy-done.1
  356.1 0.8 copy.39
  (8 shorter events, 0.1 us)
Async XLA Ops:
  257.1 96.8 %copy-start = (f32[768,768]{1,0:T(8,128)S(1)}, f32[768,768]{1,0:T(8,128)}, u32[]{:S(2)}) copy-start(f32[768,768]{1,0:T(8,128)} %get-tuple-element.25) | copy-start | bytes 7077892
  346.0 9.3 %copy-start.2 = (f32[48,3072]{1,0:T(8,128)S(1)}, f32[48,3072]{1,0:T(8,128)}, u32[]{:S(2)}) copy-start(f32[48,3072]{1,0:T(8,128)} %get-tuple-element.31) | copy-start | bytes 1769476
  346.0 10.1 %copy-start.1 = (f32[192,768]{1,0:T(8,128)S(1)}, f32[192,768]{1,0:T(8,128)}, u32[]{:S(2)}) copy-start(f32[192,768]{1,0:T(8,128)} %get-tuple-element.32) | copy-start | bytes 1769476
